TPU v7x, 128 devices: a whole 4x4x4 slice. The times are simulated.
128 devices in a mesh: gx: 4 (over x), gy: 16 (over z, y), gz: 2 (over core).
Axes of the slice: x: 4, y: 4, z: 4, core: 2. Of those that a mesh axis runs over, the one named last changes fastest.
Arguments:
- tensor: float32 [128, 1024, 128, 32], P('gx', 'gy', 'gz'), may hold values from -6 to 6
- factor_one: float32 [128, 64], P('gx'), may hold values from -0.5 to 0.5
- factor_two: float32 [1024, 64], P('gy'), may hold values from -0.1875 to 0.1875
- factor_three: float32 [128, 64], P('gz'), may hold values from -0.5 to 0.5
- species_factor: float32 [32, 16], replicated, may hold values from -1 to 1
Outputs:
- new_one: float32 [128, 64], P('gx')
- new_two: float32 [1024, 64], P('gy')
All inputs are finite; a program needn't handle non-finite values.
Results may differ from a plain program's by a relative error of at most 0.0003.
Values sent between devices are 32-bit elements; how exact they have to be, the bound alone decides.
No kernel may reach another device: no remote copies, remote signals or barrier semaphores. Data moves between devices by JAX's collectives and lax.ppermute only.
A program may use at most 192 MiB of HBM per device.

v0:
```python
import math

import jax
import jax.numpy as jnp
from jax import lax
from jax.sharding import PartitionSpec as P


def orthonormal(image, normal_matrix):
    lower = jnp.linalg.cholesky(normal_matrix)
    return jax.scipy.linalg.solve_triangular(lower, image.T, lower=True).T


def update_first(unfolded, factor_local):
    high = lax.Precision.HIGHEST
    all_rows, all_factor = (
        lax.all_gather(unfolded, "gx", axis=0, tiled=True),
        lax.all_gather(factor_local, "gx", axis=0, tiled=True),
    )
    gram_rows = lax.psum(jnp.dot(unfolded, all_rows.T, precision=high), ("gy", "gz"))
    image = jnp.dot(gram_rows, all_factor, precision=high)
    normal_matrix = lax.psum(jnp.dot(image.T, image, precision=high), "gx")
    return orthonormal(image, normal_matrix)


def update_second(unfolded, factor_local):
    high = lax.Precision.HIGHEST
    all_rows, all_factor = (
        lax.all_gather(unfolded, "gy", axis=0, tiled=True),
        lax.all_gather(factor_local, "gy", axis=0, tiled=True),
    )
    gram_rows = lax.psum(jnp.dot(unfolded, all_rows.T, precision=high), ("gx", "gz"))
    image = jnp.dot(gram_rows, all_factor, precision=high)
    normal_matrix = lax.psum(jnp.dot(image.T, image, precision=high), "gy")
    return orthonormal(image, normal_matrix)


def per_device(tensor, factor_one, factor_two, factor_three, species_factor):
    high = lax.Precision.HIGHEST
    species_cut = jnp.einsum("abcs,sq->abcq", tensor, species_factor, precision=high)
    core_local = jnp.einsum("abcq,cr->abrq", species_cut, factor_three, precision=high)
    core_local = core_local.reshape(core_local.shape[0], core_local.shape[1], -1)
    core_cut = lax.psum_scatter(core_local, "gz", scatter_dimension=2, tiled=True)
    first_local = jnp.einsum("abk,bp->apk", core_cut, factor_two, precision=high)
    first_proj = lax.psum_scatter(first_local, "gy", scatter_dimension=1, tiled=True)
    first_unf = first_proj.reshape(first_proj.shape[0], -1)
    basis_one = update_first(first_unf, factor_one)
    second_local = jnp.einsum("abk,ap->bpk", core_cut, basis_one, precision=high)
    second_proj = lax.psum_scatter(second_local, "gx", scatter_dimension=1, tiled=True)
    second_unf = second_proj.reshape(second_proj.shape[0], -1)
    basis_two = update_second(second_unf, factor_two)
    first_total = factor_one.shape[0] * lax.axis_size("gx")
    second_total = factor_two.shape[0] * lax.axis_size("gy")
    return (basis_one * math.sqrt(first_total), basis_two * math.sqrt(second_total))


def solution(mesh):
    in_specs = (P("gx", "gy", "gz", None), P("gx", None), P("gy", None), P("gz", None), P())
    out_specs = (P("gx", None), P("gy", None))
    return jax.shard_map(
        per_device, mesh=mesh, in_specs=in_specs, out_specs=out_specs, check_vma=False
    )
```

profile of v0, /device:TPU:1, one launch (start us, length us, event | category | flops | bytes accessed | tf_op | source)
XLA Modules:
  0.0 842.3 jit_solution(5682627114756535832)
XLA Ops:
  7.2 0.0 reduce-scatter.4.cloned.1.call-start
  7.2 24.2 %fusion.15 = f32[32,64,64,16]{2,3,1,0:T(8,128)S(1)} fusion(f32[32,64,64,32]{2,3,1,0:T(8,128)} %param.6, f32[32,16]{0,1:T(8,128)} %param.10), kind=kOutput, calls=%fused_computation.25 | convolution fusion | flops 805306368 | bytes 25167872 | tf_op jit(solution)/shard_map/abcs,sq->abcq/dot_general | solution.py:40
  31.5 17.4 %fusion.2 = f32[32,64,64,16]{2,1,3,0:T(8,128)} fusion(f32[32,64,64,16]{2,3,1,0:T(8,128)S(1)} %fusion.15, f32[64,64]{1,0:T(8,128)S(1)} %copy-done), kind=kOutput, calls=%fused_computation.2 | convolution fusion | flops 1610612736 | bytes 16793600 | tf_op jit(solution)/shard_map/abcq,cr->abrq/dot_general | solution.py:41
  48.8 18.3 %copy.32 = f32[32,64,64,16]{1,3,2,0:T(8,128)} copy(f32[32,64,64,16]{2,1,3,0:T(8,128)} %fusion.2) | data formatting | bytes 16777216 | tf_op jit(solution)/shard_map/abcq,cr->abrq/transpose | solution.py:41
  67.1 0.0 reduce-scatter.4.cloned.1.call-update
  67.1 0.2 reduce-scatter.6.cloned.1.call-start
  67.3 32.5 %reduce-scatter.4.cloned.1.call-done = f32[32,64,512]{1,2,0:T(8,128)} async-done(((f32[32,64,1024]{1,2,0:T(8,128)}), f32[32,64,512]{1,2,0:T(8,128)}) %reduce-scatter.4.cloned.1.call-update) | async-done | bytes 4194320 | tf_op jit(solution)/shard_map/reduce_scatter | solution.py:43
  99.9 12.3 %convolution_bitcast_fusion.1 = f32[32,64,512]{2,1,0:T(8,128)S(1)} fusion(f32[32,64,512]{1,2,0:T(8,128)} %reduce-scatter.4.cloned.1.call-done, f32[64,64]{1,0:T(8,128)S(1)} %copy-done.3), kind=kOutput, calls=%fused_computation.4 | convolution fusion | flops 805306368 | bytes 8404992 | tf_op jit(solution)/shard_map/abk,bp->apk/dot_general | solution.py:44
  112.2 4.4 copy.35
  116.6 0.0 reduce-scatter.6.cloned.1.call-update
  116.6 0.0 all-gather.3.cloned.1.call-start
  116.6 77.3 %reduce-scatter.6.cloned.1.call-done = f32[32,4,512]{2,0,1:T(8,128)} async-done(((f32[32,64,512]{2,0,1:T(8,128)}), f32[32,4,512]{2,0,1:T(8,128)}) %reduce-scatter.6.cloned.1.call-update) | async-done | bytes 262160 | tf_op jit(solution)/shard_map/reduce_scatter | solution.py:45
  193.9 1.7 copy.49
  195.6 0.0 all-gather.3.cloned.1.call-update
  195.6 0.0 reduce-scatter.8.cloned.1.call-start
  195.7 9.3 %all_gather.13 = f32[128,64]{1,0:T(8,128)S(1)} all-gather(f32[32,64]{1,0:T(8,128)S(1)} %copy-done.4), channel_id=1, replica_groups=mesh['gx'=4,'gy'=16,'gz'=2] {'gx'}, dimensions={0}, use_global_device_ids=true | all-gather | bytes 40960 | tf_op jit(solution)/shard_map/all_gather | solution.py:18
  204.9 7.5 copy.39
  212.4 7.2 all-gather.3.cloned.1.call-done
  219.6 2.3 fusion.17
  222.0 123.3 %psum.28 = f32[32,128]{1,0:T(8,128)S(1)} all-reduce(f32[32,128]{1,0:T(8,128)S(1)} %fusion.17), channel_id=1, replica_groups=mesh['gx'=4,'gy'=16,'gz'=2] {'gy','gz'}, use_global_device_ids=true, to_apply=%region_2.0 | all-reduce | flops 4096 | bytes 32768 | tf_op jit(solution)/shard_map/psum | solution.py:20
  345.3 0.2 fusion.18
  345.5 0.3 fusion.19
  345.7 12.1 %psum.29 = f32[64,64]{0,1:T(8,128)S(1)} all-reduce(f32[64,64]{0,1:T(8,128)S(1)} %fusion.19), channel_id=1, replica_groups=mesh['gx'=4,'gy'=16,'gz'=2] {'gx'}, use_global_device_ids=true, to_apply=%region_3.0 | all-reduce | flops 4096 | bytes 32768 | tf_op jit(solution)/shard_map/psum | solution.py:22
  357.8 0.1 copy.38
  357.9 5.8 cholesky.44
  363.8 0.6 compare_reduce_fusion.1
  364.4 0.7 fusion.5
  365.1 4.9 custom-call.10
  370.0 0.2 fusion.10
  370.2 10.6 %convolution_bitcast_fusion = f32[64,64,512]{2,1,0:T(8,128)} fusion(f32[32,64,512]{2,0,1:T(8,128)} %copy.39, f32[64,32]{0,1:T(8,128)S(1)} %fusion.10), kind=kOutput, calls=%fused_computation.3 | convolution fusion | flops 805306368 | bytes 12591104 | tf_op jit(solution)/shard_map/abk,ap->bpk/dot_general | solution.py:48
  380.8 0.0 all-gather.5.cloned.1.call-start
  380.9 84.1 %reduce-scatter.8.cloned.1.call-done = f32[64,16,512]{2,1,0:T(8,128)} async-done(((f32[64,64,512]{2,1,0:T(8,128)}), f32[64,16,512]{2,1,0:T(8,128)}) %reduce-scatter.8.cloned.1.call-update) | async-done | bytes 2097168 | tf_op jit(solution)/shard_map/reduce_scatter | solution.py:49
  464.9 4.1 copy.50
  469.1 0.0 all-reduce.2.cloned.1.call-start
  469.1 21.1 %all_gather.15 = f32[1024,64]{1,0:T(8,128)S(1)} all-gather(f32[64,64]{1,0:T(8,128)S(1)} %copy-done.3), channel_id=1, replica_groups=mesh['gx'=4,'gy'=16,'gz'=2] {'gy'}, dimensions={0}, use_global_device_ids=true | all-gather | bytes 278528 | tf_op jit(solution)/shard_map/all_gather | solution.py:30
  490.2 177.0 %all-gather.5.cloned.1.call-done = f32[1024,8192]{1,0:T(8,128)} async-done(((f32[64,8192]{1,0:T(8,128)}), f32[1024,8192]{1,0:T(8,128)}) %all-gather.5.cloned.1.call-update) | async-done | bytes 33554448 | tf_op jit(solution)/shard_map/all_gather | solution.py:29
  667.2 35.7 %fusion.20 = f32[64,1024]{1,0:T(8,128)} fusion(f32[64,8192]{1,0:T(8,128)} %bitcast.66, f32[1024,8192]{1,0:T(8,128)} %all-gather.5.cloned.1.call-done), kind=kOutput, calls=%fused_computation.32 | convolution fusion | flops 6442450944 | bytes 35913728 | tf_op jit(solution)/shard_map/dot_general | solution.py:32
  702.9 0.6 multiply_bitcast_fusion
  703.5 56.8 %all-reduce.2.cloned.1.call-done = f32[64,1024]{1,0:T(8,128)} async-done(((f32[64,1024]{1,0:T(8,128)}), f32[64,1024]{1,0:T(8,128)}) %all-reduce.2.cloned.1.call-update) | async-done | bytes 262160 | tf_op jit(solution)/shard_map/psum | solution.py:32
  760.3 1.4 fusion.21
  761.7 0.2 fusion.22
  761.9 60.5 %psum.31 = f32[64,64]{0,1:T(8,128)S(1)} all-reduce(f32[64,64]{0,1:T(8,128)S(1)} %fusion.22), channel_id=1, replica_groups=mesh['gx'=4,'gy'=16,'gz'=2] {'gy'}, use_global_device_ids=true, to_apply=%region_8.10 | all-reduce | flops 4096 | bytes 32768 | tf_op jit(solution)/shard_map/psum | solution.py:34
  822.5 0.1 copy.41
  822.5 5.8 cholesky.55
  828.4 0.6 compare_reduce_fusion
  829.1 0.7 fusion.6
  829.7 4.9 custom-call.11
  834.6 0.8 convolution_multiply_fusion
  (17 shorter events, 0.2 us)
Async XLA Ops:
  7.2 24.3 %copy-start = (f32[64,64]{1,0:T(8,128)S(1)}, f32[64,64]{1,0:T(8,128)}, u32[]{:S(2)}) copy-start(f32[64,64]{1,0:T(8,128)} %param.9) | copy-start | bytes 49156
  7.2 92.7 %reduce-scatter.4.cloned.1.call-start = ((), (), s32[]{:S(2)}) async-start(), calls=%async_computation.3 | async-start | bytes 25165824 | tf_op jit(solution)/shard_map/reduce_scatter | solution.py:43
  67.1 32.8 %copy-start.3 = (f32[64,64]{1,0:T(8,128)S(1)}, f32[64,64]{1,0:T(8,128)}, u32[]{:S(2)}) copy-start(f32[64,64]{1,0:T(8,128)} %param.8) | copy-start | bytes 49156
  67.1 126.8 %reduce-scatter.6.cloned.1.call-start = ((), (), s32[]{:S(2)}) async-start(), calls=%async_computation.4 | async-start | bytes 4456448 | tf_op jit(solution)/shard_map/reduce_scatter | solution.py:45
  112.2 83.5 %copy-start.4 = (f32[32,64]{1,0:T(8,128)S(1)}, f32[32,64]{1,0:T(8,128)}, u32[]{:S(2)}) copy-start(f32[32,64]{1,0:T(8,128)} %param.7) | copy-start | bytes 24580
  116.6 103.0 %all-gather.3.cloned.1.call-start = ((), (), s32[]{:S(2)}) async-start(), calls=%async_computation.5 | async-start | bytes 1310720 | tf_op jit(solution)/shard_map/all_gather | solution.py:17
  195.6 24.0 %copy-start.2 = (f32[4,4,8,512]{3,2,0,1:T(8,128)S(1)}, f32[4,4,8,512]{3,2,0,1:T(8,128)}, u32[]{:S(2)}) copy-start(f32[4,4,8,512]{3,2,0,1:T(8,128)} %copy.49) | copy-start | bytes 786436
  195.6 269.3 %reduce-scatter.8.cloned.1.call-start = ((), (), s32[]{:S(2)}) async-start(), calls=%async_computation.6 | async-start | bytes 10485760 | tf_op jit(solution)/shard_map/reduce_scatter | solution.py:49
  380.8 286.4 %all-gather.5.cloned.1.call-start = ((), (), s32[]{:S(2)}) async-start(), calls=%async_computation.7 | async-start | bytes 35651584 | tf_op jit(solution)/shard_map/all_gather | solution.py:29
  469.1 291.2 %all-reduce.2.cloned.1.call-start = ((), (), s32[]{:S(2)}) async-start(), calls=%async_computation.8 | async-start | bytes 524288 | tf_op jit(solution)/shard_map/psum | solution.py:32
  667.2 168.2 %copy-start.1 = (f32[64,64]{1,0:T(8,128)S(1)}, f32[64,64]{1,0:T(8,128)}, u32[]{:S(2)}) copy-start(f32[64,64]{1,0:T(8,128)} %param.9) | copy-start | bytes 49156
Sparse Core Ops, SparseCore 0:
  67.2 32.6 reduce-scatter.3
  116.7 77.1 reduce-scatter.5
  195.7 23.8 all-gather.2
  380.9 83.9 reduce-scatter.7
  469.2 197.9 all-gather.4
  703.0 57.2 all-reduce.1
where the time goes:
time: 858 us; the launch traced here: 842 us
  waiting for transfers between devices  435 us (51%)
  blocking collectives  226 us (26%)
  matrix products  106 us (12%)
  local copies, waits for them, and re-layouts  36 us (4%)
  other arithmetic  24.8 us (3%)
  between operations  14.3 us (2%)
    all_gather x1, waiting for transfers between devices, update_second(): lax.all_gather(unfolded, 'gy', axis=0, tiled=True)  177 us
    psum x1, blocking collectives, update_first(): lax.psum(jnp.dot(unfolded, all_rows.T, precision=high), ('gy', 'gz'))  123 us
    reduce_scatter x1, waiting for transfers between devices, per_device(): lax.psum_scatter(second_local, 'gx', scatter_dimension=1, tiled=True)  84.1 us
    reduce_scatter x1, waiting for transfers between devices, per_device(): lax.psum_scatter(first_local, 'gy', scatter_dimension=1, tiled=True)  77.3 us
    psum x1, blocking collectives, update_second(): normal_matrix = lax.psum(jnp.dot(image.T, image, precision=high), 'gy')  60.5 us
    psum x1, waiting for transfers between devices, update_second(): lax.psum(jnp.dot(unfolded, all_rows.T, precision=high), ('gx', 'gz'))  56.8 us
    dot_general x1, matrix products, update_second(): jnp.dot(unfolded, all_rows.T, precision=high)  35.7 us
    reduce_scatter x1, waiting for transfers between devices, per_device(): lax.psum_scatter(core_local, 'gz', scatter_dimension=2, tiled=True)  32.5 us
  transfers between devices with their start and end apart: 6, of which 6 were waited for; matrix products, arithmetic and copies ran while one was open for 1% of the time, Pallas kernels for 0%

commit v1 on v0

v1 whole, which is shorter than its diff:
```python
import functools
import math

import jax
import jax.numpy as jnp
from jax import lax
from jax.experimental import pallas as pl
from jax.experimental.pallas import tpu as pltpu
from jax.sharding import PartitionSpec as P

F32, BF16 = jnp.float32, jnp.bfloat16
NN = (((1,), (0,)), ((), ()))
NT = (((1,), (1,)), ((), ()))
TN = (((0,), (0,)), ((), ()))
ALL = ("gx", "gy", "gz")
PAIRS = 8
VMEM = pl.BlockSpec(memory_space=pltpu.VMEM)
PARAMS = pltpu.CompilerParams(vmem_limit_bytes=48 << 20)


def split(x):
    hi = x.astype(BF16)
    return hi, (x - hi.astype(F32)).astype(BF16)


def mm(a, b, dims):
    return lax.dot_general(a, b, dims, preferred_element_type=F32)


def mm3(a, b, dims):
    return mm(a[0], b[0], dims) + (mm(a[0], b[1], dims) + mm(a[1], b[0], dims))


def mm_f32(a, b, dims):
    return mm3(split(a), split(b), dims)


def wide(w):
    zero = jnp.zeros_like(w[0])
    return jnp.concatenate([jnp.concatenate(w, 1), jnp.concatenate([w[0], zero], 1)], 0)


def mm_wide(x, w):
    y = mm(jnp.concatenate(split(x), 1), w, NN)
    return y[:, :128] + y[:, 128:]


def iota(shape, dim):
    return lax.broadcasted_iota(jnp.int32, shape, dim)


def ones_where(mask):
    return jnp.where(mask, 1.0, 0.0).astype(BF16)


def spread(left, x, right, mask):
    return tuple(
        jnp.where(mask, mm(mm(left, part, NN).astype(BF16), right, NN), 0.0).astype(BF16)
        for part in split(x)
    )


def core_kernel(first, gz_ref, t_hbm, sft_ref, f3_ref, own_ref, peer_ref, t_vmem, xs_ref, sems):
    def copy(i):
        return pltpu.make_async_copy(t_hbm.at[pl.ds(2 * (first + i), 2)], t_vmem.at[i], sems.at[i])

    for i in range(PAIRS):
        copy(i).start()

    q = (iota((128, 16), 0) // 8 + 8 * gz_ref[0]) % 16
    rows = ones_where(q == iota((128, 16), 1))
    columns = ones_where(iota((32, 256), 0) == iota((32, 256), 1) % 32)
    same = iota((128, 256), 0) % 8 == iota((128, 256), 1) // 32
    sf = spread(rows, sft_ref[...], columns, same)
    rows = ones_where(iota((128, 64), 0) % 64 == iota((128, 64), 1))
    r = iota((64, 128), 1) // 8 * 4 + iota((64, 128), 1) % 4
    columns = ones_where(iota((64, 128), 0) == r)
    same = iota((128, 128), 0) // 64 == iota((128, 128), 1) // 4 % 2
    w3 = wide(spread(rows, f3_ref[...], columns, same))

    def pair(i, _):
        copy(i).wait()
        for g in range(8):
            at = slice(g * 8, g * 8 + 8)
            t = [t_vmem[i, a, at].reshape(256, 64) for a in range(2)]
            th, tl = split(jnp.concatenate(t, 1))
            y = mm(sf[0], jnp.concatenate([th, tl], 1), NN)
            x = y[:, :128] + y[:, 128:] + mm(sf[1], th, NN)
            xs_ref[:, at, :] = x.reshape(16, 8, 128)
        for k in range(8):
            o = mm_wide(xs_ref[2 * k : 2 * k + 2].reshape(128, 128), w3)
            o = o.T.reshape(16, 8, 128)
            if k < 4:
                own_ref[:, k, i] = o
            else:
                peer_ref[:, k - 4, i] = o
        return 0

    lax.fori_loop(0, PAIRS, pair, 0)


def core_cut(first, gz, tensor, sft, f3):
    part = jax.ShapeDtypeStruct((16, 4, PAIRS, 8, 128), F32)
    return pl.pallas_call(
        functools.partial(core_kernel, first),
        in_specs=[pl.BlockSpec(memory_space=pltpu.SMEM), pl.BlockSpec(memory_space=pl.ANY), VMEM, VMEM],
        out_specs=[VMEM, VMEM],
        out_shape=[part, part],
        scratch_shapes=[
            pltpu.VMEM((PAIRS, 2, 64, 32, 64), F32),
            pltpu.VMEM((16, 64, 128), F32),
            pltpu.SemaphoreType.DMA((PAIRS,)),
        ],
        compiler_params=PARAMS,
    )(gz, tensor, sft, f3)


def first_kernel(c_ref, e_ref, gram_ref, fp_ref, g_ref):
    step = pl.program_id(0)

    @pl.when(step == 0)
    def _():
        fp_ref[...] = jnp.zeros_like(fp_ref)

    low = iota((8, 128), 1) < 64
    total = fp_ref[...]
    for y in range(4):
        top, bottom = [], []
        for x in range(4):
            f2 = c_ref[x, y, 128:]
            turned = pltpu.roll(f2, 64, 1)
            top += [jnp.where(low, f2, 0.0), jnp.where(low, turned, 0.0)]
            bottom += [jnp.where(low, 0.0, turned), jnp.where(low, 0.0, f2)]
        w = wide(split(jnp.concatenate(top + bottom, 0)))
        total += mm_wide(c_ref[:, y, :128].reshape(512, 128), w)
    fp_ref[...] = total

    @pl.when(step == pl.num_programs(0) - 1)
    def _():
        gram, cross = jnp.zeros((128, 128), F32), jnp.zeros((128, 128), F32)
        for r in range(4):
            e = fp_ref[pl.ds(r, 128, stride=4), :]
            e_ref[:, r * 128 : (r + 1) * 128] = e
            eh, el = split(e)
            gram += mm(eh, eh, NT)
            cross += mm(eh, el, NT)
        g_ref[...] = gram + (cross + cross.T)
        group = iota((32, 128), 1) // 32
        rows = [g_ref[pl.ds(i, 32, stride=4), :] for i in range(4)]
        for x in range(4):
            block = jnp.zeros((32, 128), F32)
            for i in range(4):
                moved = pltpu.roll(rows[i], 32 * ((i - x) % 4), 1) if i != x else rows[i]
                block = jnp.where(group == i, moved, block)
            gram_ref[x] = block


def first_gram(c):
    return pl.pallas_call(
        first_kernel,
        grid=(4,),
        in_specs=[
            pl.BlockSpec((4, 4, 136, 128), lambda i: (0, i, 0, 0)),
        ],
        out_specs=[
            pl.BlockSpec((128, 512), lambda i: (0, 0)),
            pl.BlockSpec((4, 32, 128), lambda i: (0, 0, 0)),
        ],
        out_shape=[jax.ShapeDtypeStruct((128, 512), F32), jax.ShapeDtypeStruct((4, 32, 128), F32)],
        scratch_shapes=[pltpu.VMEM((512, 128), F32), pltpu.VMEM((128, 128), F32)],
        compiler_params=PARAMS,
    )(c)


def rows_kernel(parts_ref, f1_ref, out_ref):
    row = jnp.sum(parts_ref[...], axis=0, keepdims=True)
    block = jnp.concatenate([row[:, i * 32 : (i + 1) * 32] for i in range(4)] * 2, 0)
    image = mm_f32(block, f1_ref[...], NN)
    image = jnp.concatenate([image[i : i + 1] for i in range(4)], 1)
    out_ref[...] = jnp.broadcast_to(image[None], out_ref.shape)


def image_rows(parts, f1):
    return pl.pallas_call(
        rows_kernel,
        in_specs=[VMEM, VMEM],
        out_specs=VMEM,
        out_shape=jax.ShapeDtypeStruct((128, 1, 256), F32),
        compiler_params=PARAMS,
    )(parts, f1)


def sum_kernel(parts_ref, out_ref):
    out_ref[...] = jnp.broadcast_to(jnp.sum(parts_ref[...], axis=0, keepdims=True), out_ref.shape)


def sum_for_all(parts):
    return pl.pallas_call(
        sum_kernel,
        in_specs=[VMEM],
        out_specs=VMEM,
        out_shape=jax.ShapeDtypeStruct(parts.shape, F32),
        compiler_params=PARAMS,
    )(parts)


def inverse_factor(normal):
    rows, lanes = iota((64, 128), 0), iota((64, 128), 1)
    m = jnp.concatenate([normal, jnp.where(rows == lanes, 1.0, 0.0)[:, :64].astype(F32)], 1)
    for j in range(63):
        row = m[j : j + 1, :]
        column = jnp.where(rows > j, jnp.broadcast_to(m[:, j : j + 1], (64, 128)), 0.0)
        pivot = jnp.broadcast_to(m[j : j + 1, j : j + 1], (1, 128))
        m = m - column * (row / pivot)
    diagonal = jnp.sum(jnp.where(rows == lanes, m, 0.0), axis=1, keepdims=True)
    return m[:, 64:] * lax.rsqrt(diagonal)


def second_kernel(parts_ref, e_ref, c_ref, new_ref, part_ref, i_ref, y_ref, c_vmem, sem):
    copy = pltpu.make_async_copy(c_ref.at[:, :, pl.ds(0, 128)], c_vmem, sem)
    copy.start()
    rows = jnp.sum(parts_ref[...].reshape(4, 32, 256), axis=0)
    for i in range(4):
        i_ref[pl.ds(i, 32, stride=4), :] = rows[:, i * 64 : (i + 1) * 64]
    image = i_ref[...]
    normal = mm_f32(image, image, TN)
    basis = mm_f32(image, inverse_factor(normal), NT)
    new_ref[...] = basis * math.sqrt(128)
    y = mm_f32(mm_f32(basis, basis, NT), e_ref[...], NN)
    for r in range(4):
        y_ref[pl.ds(r, 128, stride=4), :] = y[:, r * 128 : (r + 1) * 128]
    yt = split(y_ref[...].T)
    low = iota((64, 128), 1) < 64
    copy.wait()

    def both(i, _):
        halves = []
        for k in range(2):
            c = split(c_vmem[:, 2 * i + k].reshape(512, 128))
            o = mm3(yt, c, NN)
            halves.append(o[:64, :] + pltpu.roll(o[64:, :], 64, 1))
        part_ref[i] = jnp.where(low, halves[0], pltpu.roll(halves[1], 64, 1))
        return 0

    lax.fori_loop(0, 8, both, 0)


def second_image(parts, e, c):
    return pl.pallas_call(
        second_kernel,
        in_specs=[VMEM, VMEM, pl.BlockSpec(memory_space=pl.ANY)],
        out_specs=[VMEM, VMEM],
        out_shape=[jax.ShapeDtypeStruct((128, 64), F32), jax.ShapeDtypeStruct((8, 64, 128), F32)],
        scratch_shapes=[
            pltpu.VMEM((128, 64), F32),
            pltpu.VMEM((512, 128), F32),
            pltpu.VMEM((4, 16, 128, 128), F32),
            pltpu.SemaphoreType.DMA,
        ],
        compiler_params=PARAMS,
    )(parts, e, c)


def last_kernel(at_ref, image_ref, new_ref):
    normal, cross = jnp.zeros((64, 64), F32), jnp.zeros((64, 64), F32)
    for i in range(8):
        h, l = split(image_ref[i])
        normal += mm(h, h, NT)
        cross += mm(h, l, NT)
    inverse = inverse_factor(normal + (cross + cross.T))
    pair = image_ref[at_ref[0]]
    mine = jnp.where(at_ref[1] == 0, pair[:, :64], pair[:, 64:])
    new_ref[...] = mm_f32(mine, inverse, (((0,), (1,)), ((), ()))) * math.sqrt(1024)


def last_factor(at, image):
    return pl.pallas_call(
        last_kernel,
        in_specs=[pl.BlockSpec(memory_space=pltpu.SMEM), VMEM],
        out_specs=VMEM,
        out_shape=jax.ShapeDtypeStruct((64, 64), F32),
        compiler_params=PARAMS,
    )(at, image)


def to_all(x, names=ALL):
    return lax.all_to_all(x, names, 0, 0, tiled=True)


def swap(x):
    return lax.ppermute(x, "gz", [(0, 1), (1, 0)])


def per_device(tensor, factor_one, factor_two, factor_three, species_factor):
    gx, gy, gz = (lax.axis_index(name).astype(jnp.int32) for name in ALL)

    t = tensor.transpose(0, 1, 3, 2)
    parts = [core_cut(i * PAIRS, gz[None], t, species_factor.T, factor_three) for i in range(2)]
    core = jnp.concatenate([own + swap(peer) for own, peer in parts], axis=2)
    f2 = lax.dynamic_slice_in_dim(factor_two, gx * 16, 16)
    f2 = jnp.broadcast_to(jnp.concatenate([f2[:8], f2[8:]], 1)[None], (64, 8, 128))
    sent = jnp.concatenate([core.reshape(64, 128, 128), f2], 1)
    c = to_all(sent, ("gx", "gy")).reshape(4, 16, 136, 128)

    e, gram = first_gram(c)
    rows = image_rows(to_all(gram.reshape(128, 1, 128)).reshape(128, 128), factor_one)
    new_one, second_part = second_image(to_all(rows).reshape(128, 256), e, c)
    second = to_all(sum_for_all(to_all(second_part.reshape(128, 4, 128)))).reshape(8, 64, 128)
    new_two = last_factor(jnp.stack([gy // 2, gy % 2]), second)
    return lax.dynamic_slice_in_dim(new_one, gx * 32, 32), new_two


def solution(mesh):
    in_specs = (P("gx", "gy", "gz", None), P("gx", None), P("gy", None), P("gz", None), P())
    out_specs = (P("gx", None), P("gy", None))
    return jax.shard_map(
        per_device, mesh=mesh, in_specs=in_specs, out_specs=out_specs, check_vma=False
    )
```

time: 858 us -> 183 us (0.21); the launches traced: 842 us -> 183 us
  waiting for transfers between devices: 435 us -> 11 us
  blocking collectives: 226 us -> 113 us
  matrix products: 106 us -> 0 us
  Pallas kernels: 0 us -> 42.1 us
  local copies, waits for them, and re-layouts: 36 us -> 4.1 us
  other arithmetic: 24.8 us -> 5.74 us
  between operations: 14.3 us -> 0.78 us
    psum x3 -> x0, blocking collectives: 196 us -> none  [the longest x1 123 us: update_first(): lax.psum(jnp.dot(unfolded, all_rows.T, precision=high), ('gy', 'gz'))]
    reduce_scatter x3 -> x0, waiting for transfers between devices: 194 us -> none  [the longest x1 84.1 us: per_device(): lax.psum_scatter(second_local, 'gx', scatter_dimension=1, tiled=True)]
    all_gather x2 -> x0, waiting for transfers between devices: 184 us -> none  [the longest x1 177 us: update_second(): lax.all_gather(unfolded, 'gy', axis=0, tiled=True)]
    all_to_all x0 -> x4, blocking collectives: none -> 113 us  [to_all(): return lax.all_to_all(x, names, 0, 0, tiled=True)]
    dot_general x10 -> x0, matrix products: 105 us -> none  [the longest x1 35.7 us: update_second(): jnp.dot(unfolded, all_rows.T, precision=high)]
    psum x1 -> x0, waiting for transfers between devices: 56.8 us -> none  [update_second(): lax.psum(jnp.dot(unfolded, all_rows.T, precision=high), ('gx', 'gz'))]
    pallas_call x0 -> x7, Pallas kernels: none -> 42.1 us  [the longest x2 19.9 us: core_cut(): pl.pallas_call(functools.partial(core_kernel, first), in_specs=[pl.BlockS...]
    all_gather x2 -> x0, blocking collectives: 30.3 us -> none  [the longest x1 21.1 us: update_second(): lax.all_gather(factor_local, 'gy', axis=0, tiled=True)]
  transfers between devices with their start and end apart: 6 -> 3, of which waited for: 6 -> 2; matrix products, arithmetic and copies ran while one was open for 1% -> 2% of each run, Pallas kernels for 0% -> 5%
where the time goes in v1:
time: 183 us
  blocking collectives  113 us (62%)
  Pallas kernels  42.1 us (23%)
  waiting for transfers between devices  11 us (6%)
  starting transfers between devices  6.16 us (3%)
  other arithmetic  5.74 us (3%)
  local copies, waits for them, and re-layouts  4.1 us (2%)
    all_to_all x4, blocking collectives, to_all(): return lax.all_to_all(x, names, 0, 0, tiled=True)  113 us
    pallas_call x2, Pallas kernels, core_cut(): pl.pallas_call(functools.partial(core_kernel, first), in_specs=[pl.BlockS...  19.9 us
    pallas_call x1, Pallas kernels, second_image(): pl.pallas_call(second_kernel, in_specs=[VMEM, VMEM, pl.BlockSpec(memory_s...  11 us
    all_to_all x1, waiting for transfers between devices, to_all(): return lax.all_to_all(x, names, 0, 0, tiled=True)  10.1 us
    pallas_call x1, Pallas kernels, last_factor(): pl.pallas_call(last_kernel, in_specs=[pl.BlockSpec(memory_space=pltpu.SME...  7.06 us
    add x2, other arithmetic, per_device(): core = jnp.concatenate([own + swap(peer) for own, peer in parts], axis=2)  4.75 us
    all_to_all x1, starting transfers between devices, to_all(): return lax.all_to_all(x, names, 0, 0, tiled=True)  4.65 us
  transfers between devices with their start and end apart: 3, of which 2 were waited for; matrix products, arithmetic and copies ran while one was open for 2% of the time, Pallas kernels for 5%

profile of v1, /device:TPU:1, one launch (start us, length us, event | category | flops | bytes accessed | tf_op | source)
XLA Modules:
  0.0 183.1 jit_solution(14877406797725310119)
XLA Ops:
  0.6 0.0 copy-start.1
  0.6 0.7 copy-done.1
  1.4 0.0 copy-start.2
  1.4 0.7 copy-done.2
  2.1 9.9 %shard_map.69 = (f32[16,4,8,8,128]{4,3,2,1,0:T(8,128)S(1)}, f32[16,4,8,8,128]{4,3,2,1,0:T(8,128)}) custom-call(s32[1]{0:T(128)} %bitcast.gz_ref, f32[32,64,32,64]{3,2,1,0:T(8,128)} %bitcast.25, f32[16,32]{1,0:T(8,128)S(1)} %bitcast.23, f32[64,64]{1,0:T(8,128)S(1)} %copy-done.1), custom_call_target="tpu_custom_call" | custom-call | tf_op jit(solution)/shard_map/pallas_call | solution.py:104
  12.0 0.0 copy-start
  12.0 1.3 copy-done
  13.3 1.4 collective-permute-start.1
  14.8 9.9 %shard_map.68 = (f32[16,4,8,8,128]{4,3,2,1,0:T(8,128)S(1)}, f32[16,4,8,8,128]{4,3,2,1,0:T(8,128)}) custom-call(s32[1]{0:T(128)} %bitcast.gz_ref, f32[32,64,32,64]{3,2,1,0:T(8,128)} %bitcast.26, f32[16,32]{1,0:T(8,128)S(1)} %bitcast.24, f32[64,64]{1,0:T(8,128)S(1)} %copy-done.1), custom_call_target="tpu_custom_call" | custom-call | tf_op jit(solution)/shard_map/pallas_call | solution.py:104
  24.7 0.1 collective-permute-start
  24.8 0.7 constant_dynamic-slice_fusion
  25.5 0.1 pad_maximum_fusion.2
  25.6 0.0 collective-permute-done.1
  25.6 2.8 %add.18 = f32[16,4,8,8,128]{4,3,2,1,0:T(8,128)S(1)} add(f32[16,4,8,8,128]{4,3,2,1,0:T(8,128)} %copy-done, f32[16,4,8,8,128]{4,3,2,1,0:T(8,128)} %collective-permute-done.1) | non-fusion elementwise | flops 524288 | bytes 6291456 | tf_op jit(solution)/shard_map/add | solution.py:299
  28.4 0.9 collective-permute-done
  29.3 2.0 %add.17 = f32[16,4,8,8,128]{4,3,2,1,0:T(8,128)S(1)} add(f32[16,4,8,8,128]{4,3,2,1,0:T(8,128)S(1)} %get-tuple-element.10, f32[16,4,8,8,128]{4,3,2,1,0:T(8,128)} %collective-permute-done) | non-fusion elementwise | flops 524288 | bytes 6291456 | tf_op jit(solution)/shard_map/add | solution.py:299
  31.3 0.5 pad_maximum_fusion.1
  31.8 0.3 pad_maximum_fusion
  32.2 65.8 %all_to_all.25 = f32[64,136,128]{2,1,0:T(8,128)S(1)} all-to-all(f32[64,136,128]{2,1,0:T(8,128)S(1)} %pad_maximum_fusion), channel_id=1, replica_groups=mesh['gx'=4,'gy'=16,'gz'=2] {'gx','gy'}, dimensions={0} | all-to-all | bytes 8912896 | tf_op jit(solution)/shard_map/all_to_all | solution.py:287
  98.0 0.0 copy-start.3
  98.0 3.0 %shard_map.70 = (f32[128,512]{1,0:T(8,128)S(1)}, f32[4,32,128]{2,1,0:T(8,128)S(1)}) custom-call(f32[4,16,136,128]{3,2,1,0:T(8,128)S(1)} %bitcast.16), custom_call_target="tpu_custom_call" | custom-call | tf_op jit(solution)/shard_map/pallas_call | solution.py:159
  101.0 17.7 %all_to_all.26 = f32[128,1,128]{2,1,0:T(1,128)S(1)} all-to-all(f32[128,1,128]{2,1,0:T(1,128)S(1)} %bitcast.22), channel_id=1, replica_groups=mesh['gx'=4,'gy'=16,'gz'=2] {'gx','gy','gz'}, dimensions={0} | all-to-all | bytes 131072 | tf_op jit(solution)/shard_map/all_to_all | solution.py:287
  118.7 0.0 copy-done.3
  118.7 0.3 shard_map.71
  119.0 14.5 %all_to_all.27 = f32[128,1,256]{2,1,0:T(1,128)S(1)} all-to-all(f32[128,1,256]{2,1,0:T(1,128)S(1)} %shard_map.71), channel_id=1, replica_groups=mesh['gx'=4,'gy'=16,'gz'=2] {'gx','gy','gz'}, dimensions={0} | all-to-all | bytes 262144 | tf_op jit(solution)/shard_map/all_to_all | solution.py:287
  133.5 11.0 %shard_map.72 = (f32[128,64]{1,0:T(8,128)S(1)}, f32[8,64,128]{2,1,0:T(8,128)S(1)}) custom-call(f32[128,256]{1,0:T(8,128)S(1)} %bitcast.19, f32[128,512]{1,0:T(8,128)S(1)} %get-tuple-element.15.e_ref, f32[4,16,136,128]{3,2,1,0:T(8,128)S(1)} %bitcast.17), custom_call_target="tpu_custom_call" | custom-call | tf_op jit(solution)/shard_map/pallas_call | solution.py:249
  144.6 15.1 %all_to_all.28.parts_ref = f32[128,4,128]{2,1,0:T(4,128)S(1)} all-to-all(f32[128,4,128]{2,1,0:T(4,128)S(1)} %bitcast.20), channel_id=1, replica_groups=mesh['gx'=4,'gy'=16,'gz'=2] {'gx','gy','gz'}, dimensions={0} | all-to-all | bytes 524288 | tf_op jit(solution)/shard_map/all_to_all | solution.py:287
  159.7 0.9 shard_map.73
  160.6 4.6 %all-to-all-start.4 = ((f32[128,4,128]{2,1,0:T(4,128)}), f32[128,4,128]{2,1,0:T(4,128)S(1)}, u32[]{:S(2)}, u32[]{:S(2)}) async-start(f32[128,4,128]{2,1,0:T(4,128)} %shard_map.73), calls=%async_computation.4 | async-start | bytes 524288 | tf_op jit(solution)/shard_map/all_to_all | solution.py:287
  165.2 0.1 pad_add_fusion.at_ref
  165.3 0.6 constant_dynamic-slice_fusion.1
  165.9 10.1 %all-to-all-done.4 = f32[128,4,128]{2,1,0:T(4,128)S(1)} async-done(((f32[128,4,128]{2,1,0:T(4,128)}), f32[128,4,128]{2,1,0:T(4,128)S(1)}, u32[]{:S(2)}, u32[]{:S(2)}) %all-to-all-start.4) | async-done | bytes 262176 | tf_op jit(solution)/shard_map/all_to_all | solution.py:287
  176.0 7.1 %shard_map.74 = f32[64,64]{1,0:T(8,128)} custom-call(s32[2]{0:T(128)S(1)} %pad_add_fusion.at_ref, f32[8,64,128]{2,1,0:T(8,128)S(1)} %bitcast.18), custom_call_target="tpu_custom_call" | custom-call | tf_op jit(solution)/shard_map/pallas_call | solution.py:277
  (2 shorter events, 0.0 us)
Async XLA Ops:
  0.6 0.8 copy-start.1
  1.4 0.7 copy-start.2
  12.0 1.3 copy-start
  13.3 12.3 %collective-permute-start.1 = (f32[16,4,8,8,128]{4,3,2,1,0:T(8,128)}, f32[16,4,8,8,128]{4,3,2,1,0:T(8,128)}, u32[]{:S(2)}, u32[]{:S(2)}) collective-permute-start(f32[16,4,8,8,128]{4,3,2,1,0:T(8,128)} %get-tuple-element.13), channel_id=1, source_target_pairs={{0,1},{1,0},{2,3},{3,2},{4,5},{5,4},{6,7},{7,6},{8,9},{9,8},{10,11... | collective-permute-start | bytes 6291464 | tf_op jit(solution)/shard_map/ppermute | solution.py:291
  24.7 4.6 %collective-permute-start = (f32[16,4,8,8,128]{4,3,2,1,0:T(8,128)}, f32[16,4,8,8,128]{4,3,2,1,0:T(8,128)}, u32[]{:S(2)}, u32[]{:S(2)}) collective-permute-start(f32[16,4,8,8,128]{4,3,2,1,0:T(8,128)} %get-tuple-element.11), channel_id=1, source_target_pairs={{0,1},{1,0},{2,3},{3,2},{4,5},{5,4},{6,7},{7,6},{8,9},{9,8},{10,11... | collective-permute-start | bytes 6291464 | tf_op jit(solution)/shard_map/ppermute | solution.py:291
  98.0 20.7 %copy-start.3 = (f32[32,64]{1,0:T(8,128)S(1)}, f32[32,64]{1,0:T(8,128)}, u32[]{:S(2)}) copy-start(f32[32,64]{1,0:T(8,128)} %f1_ref.1) | copy-start | bytes 24580
  160.6 15.4 %all-to-all-start.4 = ((f32[128,4,128]{2,1,0:T(4,128)}), f32[128,4,128]{2,1,0:T(4,128)S(1)}, u32[]{:S(2)}, u32[]{:S(2)}) async-start(f32[128,4,128]{2,1,0:T(4,128)} %shard_map.73), calls=%async_computation.4 | async-start | bytes 524288 | tf_op jit(solution)/shard_map/all_to_all | solution.py:287

commit v2 on v1

--- a/solution.py
+++ b/solution.py
@@ -13,9 +13,13 @@
 NT = (((1,), (1,)), ((), ()))
 TN = (((0,), (0,)), ((), ()))
 ALL = ("gx", "gy", "gz")
-PAIRS = 8
+PAIRS = (12, 4)
+SLOTS = 6
 VMEM = pl.BlockSpec(memory_space=pltpu.VMEM)
-PARAMS = pltpu.CompilerParams(vmem_limit_bytes=48 << 20)
+PARAMS = pltpu.CompilerParams(vmem_limit_bytes=12 << 20)
+LARGE = pltpu.CompilerParams(vmem_limit_bytes=24 << 20)
+HBM = pl.BlockSpec(memory_space=pltpu.HBM)
+SMEM = pl.BlockSpec(memory_space=pltpu.SMEM)
 
 
 def split(x):
@@ -60,33 +64,43 @@
     )
 
 
-def core_kernel(first, gz_ref, t_hbm, sft_ref, f3_ref, own_ref, peer_ref, t_vmem, xs_ref, sems):
+def core_kernel(
+    first, pairs, gz_ref, t_hbm, factors_ref, own_hbm, peer_hbm, own_ref, peer_ref, t_vmem, xa_ref, xb_ref, sems, out_sems
+):
     def copy(i):
-        return pltpu.make_async_copy(t_hbm.at[pl.ds(2 * (first + i), 2)], t_vmem.at[i], sems.at[i])
-
-    for i in range(PAIRS):
+        slot = i % SLOTS
+        return pltpu.make_async_copy(t_hbm.at[pl.ds(2 * (first + i), 2)], t_vmem.at[slot], sems.at[slot])
+
+    def copies_out(i):
+        return [
+            pltpu.make_async_copy(ref.at[:, :, pl.ds(i, 2)], hbm.at[:, :, pl.ds(i, 2)], out_sems.at[k, i // 2])
+            for k, (ref, hbm) in enumerate(((own_ref, own_hbm), (peer_ref, peer_hbm)))
+        ]
+
+    for i in range(min(SLOTS, pairs)):
         copy(i).start()
 
-    q = (iota((128, 16), 0) // 8 + 8 * gz_ref[0]) % 16
+    q = ((iota((128, 16), 0) >> 3) + 8 * gz_ref[0]) & 15
     rows = ones_where(q == iota((128, 16), 1))
-    columns = ones_where(iota((32, 256), 0) == iota((32, 256), 1) % 32)
-    same = iota((128, 256), 0) % 8 == iota((128, 256), 1) // 32
-    sf = spread(rows, sft_ref[...], columns, same)
-    rows = ones_where(iota((128, 64), 0) % 64 == iota((128, 64), 1))
-    r = iota((64, 128), 1) // 8 * 4 + iota((64, 128), 1) % 4
+    columns = ones_where(iota((32, 256), 0) == (iota((32, 256), 1) & 31))
+    same = (iota((128, 256), 0) & 7) == (iota((128, 256), 1) >> 5)
+    sf = spread(rows, factors_ref[:16, 64:96], columns, same)
+    rows = ones_where((iota((128, 64), 0) & 63) == iota((128, 64), 1))
+    r = (iota((64, 128), 1) >> 3 << 2) + (iota((64, 128), 1) & 3)
     columns = ones_where(iota((64, 128), 0) == r)
-    same = iota((128, 128), 0) // 64 == iota((128, 128), 1) // 4 % 2
-    w3 = wide(spread(rows, f3_ref[...], columns, same))
-
-    def pair(i, _):
-        copy(i).wait()
+    same = (iota((128, 128), 0) >> 6) == ((iota((128, 128), 1) >> 2) & 1)
+    w3 = wide(spread(rows, factors_ref[:, :64], columns, same))
+
+    def contract_s(i, xs_ref):
         for g in range(8):
             at = slice(g * 8, g * 8 + 8)
-            t = [t_vmem[i, a, at].reshape(256, 64) for a in range(2)]
+            t = [t_vmem[i % SLOTS, a, at].reshape(256, 64) for a in range(2)]
             th, tl = split(jnp.concatenate(t, 1))
             y = mm(sf[0], jnp.concatenate([th, tl], 1), NN)
             x = y[:, :128] + y[:, 128:] + mm(sf[1], th, NN)
             xs_ref[:, at, :] = x.reshape(16, 8, 128)
+
+    def contract_c(i, xs_ref):
         for k in range(8):
             o = mm_wide(xs_ref[2 * k : 2 * k + 2].reshape(128, 128), w3)
             o = o.T.reshape(16, 8, 128)
@@ -94,25 +108,86 @@
                 own_ref[:, k, i] = o
             else:
                 peer_ref[:, k - 4, i] = o
+
+    def two_pairs(step, _):
+        i = 2 * step
+        copy(i).wait()
+        contract_s(i, xa_ref)
+        copy(i + 1).wait()
+        contract_s(i + 1, xb_ref)
+        contract_c(i, xa_ref)
+        contract_c(i + 1, xb_ref)
+        for out in copies_out(i):
+            out.start()
+
+        @pl.when(i + SLOTS < pairs)
+        def _():
+            copy(i + SLOTS).start()
+            copy(i + SLOTS + 1).start()
+
         return 0
 
-    lax.fori_loop(0, PAIRS, pair, 0)
-
-
-def core_cut(first, gz, tensor, sft, f3):
-    part = jax.ShapeDtypeStruct((16, 4, PAIRS, 8, 128), F32)
-    return pl.pallas_call(
-        functools.partial(core_kernel, first),
-        in_specs=[pl.BlockSpec(memory_space=pltpu.SMEM), pl.BlockSpec(memory_space=pl.ANY), VMEM, VMEM],
-        out_specs=[VMEM, VMEM],
+    lax.fori_loop(0, pairs // 2, two_pairs, 0)
+    for i in range(0, pairs, 2):
+        for out in copies_out(i):
+            out.wait()
+
+
+def core_cut(first, pairs, gz, tensor, factors):
+    part = pltpu.HBM((16, 4, pairs, 8, 128), F32)
+    return pl.pallas_call(
+        functools.partial(core_kernel, first, pairs),
+        in_specs=[SMEM, HBM, VMEM],
+        out_specs=[HBM, HBM],
         out_shape=[part, part],
         scratch_shapes=[
-            pltpu.VMEM((PAIRS, 2, 64, 32, 64), F32),
+            pltpu.VMEM((16, 4, pairs, 8, 128), F32),
+            pltpu.VMEM((16, 4, pairs, 8, 128), F32),
+            pltpu.VMEM((SLOTS, 2, 64, 32, 64), F32),
             pltpu.VMEM((16, 64, 128), F32),
-            pltpu.SemaphoreType.DMA((PAIRS,)),
+            pltpu.VMEM((16, 64, 128), F32),
+            pltpu.SemaphoreType.DMA((SLOTS,)),
+            pltpu.SemaphoreType.DMA((2, pairs // 2)),
         ],
-        compiler_params=PARAMS,
-    )(gz, tensor, sft, f3)
+        compiler_params=LARGE,
+    )(gz, tensor, factors)
+
+
+def merge_first_kernel(gx_ref, own_ref, other_ref, f2_ref, out_ref):
+    rows = 8 * PAIRS[0]
+    for g in range(16):
+        out_ref[4 * g : 4 * g + 4, :rows] = (own_ref[g] + other_ref[g]).reshape(4, rows, 128)
+    f2 = f2_ref[pl.ds(pl.multiple_of(16 * gx_ref[0], 16), 16), :]
+    f2 = jnp.concatenate([f2[:8], f2[8:]], 1)
+    out_ref[:, 128:] = jnp.broadcast_to(f2[None], (64, 8, 128))
+
+
+def merge_second_kernel(own_ref, other_ref, sent_ref, out_ref):
+    rows = 8 * PAIRS[1]
+    for g in range(16):
+        total = (own_ref[g] + other_ref[g]).reshape(4, rows, 128)
+        out_ref[4 * g : 4 * g + 4, 8 * PAIRS[0] : 128] = total
+
+
+def merge_first(gx, own, other, f2):
+    return pl.pallas_call(
+        merge_first_kernel,
+        in_specs=[SMEM, VMEM, VMEM, VMEM],
+        out_specs=VMEM,
+        out_shape=pltpu.VMEM((64, 136, 128), F32),
+        compiler_params=PARAMS,
+    )(gx, own, other, f2)
+
+
+def merge_second(own, other, sent):
+    return pl.pallas_call(
+        merge_second_kernel,
+        in_specs=[VMEM, VMEM, VMEM],
+        out_specs=VMEM,
+        out_shape=pltpu.VMEM((64, 136, 128), F32),
+        input_output_aliases={2: 0},
+        compiler_params=PARAMS,
+    )(own, other, sent)
 
 
 def first_kernel(c_ref, e_ref, gram_ref, fp_ref, g_ref):
@@ -207,11 +282,35 @@
 def inverse_factor(normal):
     rows, lanes = iota((64, 128), 0), iota((64, 128), 1)
     m = jnp.concatenate([normal, jnp.where(rows == lanes, 1.0, 0.0)[:, :64].astype(F32)], 1)
-    for j in range(63):
-        row = m[j : j + 1, :]
-        column = jnp.where(rows > j, jnp.broadcast_to(m[:, j : j + 1], (64, 128)), 0.0)
-        pivot = jnp.broadcast_to(m[j : j + 1, j : j + 1], (1, 128))
-        m = m - column * (row / pivot)
+    blocks = [m[8 * k : 8 * k + 8] for k in range(8)]
+    for k in range(8):
+        row = [blocks[k][i : i + 1] for i in range(8)]
+        pivot = {}
+        for i in range(8):
+            for l in range(i, 8):
+                entry = blocks[k][i : i + 1, 8 * k + l : 8 * k + l + 1]
+                pivot[i, l] = jnp.broadcast_to(entry, (1, 128))
+        factor, taken = {}, []
+        for i in range(8):
+            inverse = 1.0 / pivot[i, i]
+            taken.append(row[i] * inverse)
+            for l in range(i + 1, 8):
+                factor[i, l] = pivot[i, l] * inverse
+            for l in range(i + 1, 8):
+                row[l] = row[l] - pivot[i, l] * taken[i]
+                for n in range(l, 8):
+                    pivot[l, n] = pivot[l, n] - factor[i, l] * pivot[i, n]
+        for i in reversed(range(8)):
+            for l in range(i + 1, 8):
+                taken[i] = taken[i] - factor[i, l] * taken[l]
+        blocks[k] = jnp.concatenate(row, 0)
+        for t in range(k + 1, 8):
+            rest = blocks[t]
+            for i in range(8):
+                at = 8 * k + i
+                rest = rest - jnp.broadcast_to(blocks[t][:, at : at + 1], (8, 128)) * taken[i]
+            blocks[t] = rest
+    m = jnp.concatenate(blocks, 0)
     diagonal = jnp.sum(jnp.where(rows == lanes, m, 0.0), axis=1, keepdims=True)
     return m[:, 64:] * lax.rsqrt(diagonal)
 
@@ -224,9 +323,11 @@
         i_ref[pl.ds(i, 32, stride=4), :] = rows[:, i * 64 : (i + 1) * 64]
     image = i_ref[...]
     normal = mm_f32(image, image, TN)
-    basis = mm_f32(image, inverse_factor(normal), NT)
+    projected = split(mm_f32(image, e_ref[...], TN))
+    inverse = split(inverse_factor(normal))
+    basis = mm3(split(image), inverse, NT)
     new_ref[...] = basis * math.sqrt(128)
-    y = mm_f32(mm_f32(basis, basis, NT), e_ref[...], NN)
+    y = mm_f32(basis, mm3(inverse, projected, NN), NN)
     for r in range(4):
         y_ref[pl.ds(r, 128, stride=4), :] = y[:, r * 128 : (r + 1) * 128]
     yt = split(y_ref[...].T)
@@ -248,7 +349,7 @@
 def second_image(parts, e, c):
     return pl.pallas_call(
         second_kernel,
-        in_specs=[VMEM, VMEM, pl.BlockSpec(memory_space=pl.ANY)],
+        in_specs=[VMEM, VMEM, HBM],
         out_specs=[VMEM, VMEM],
         out_shape=[jax.ShapeDtypeStruct((128, 64), F32), jax.ShapeDtypeStruct((8, 64, 128), F32)],
         scratch_shapes=[
@@ -276,7 +377,7 @@
 def last_factor(at, image):
     return pl.pallas_call(
         last_kernel,
-        in_specs=[pl.BlockSpec(memory_space=pltpu.SMEM), VMEM],
+        in_specs=[SMEM, VMEM],
         out_specs=VMEM,
         out_shape=jax.ShapeDtypeStruct((64, 64), F32),
         compiler_params=PARAMS,
@@ -294,12 +395,12 @@
 def per_device(tensor, factor_one, factor_two, factor_three, species_factor):
     gx, gy, gz = (lax.axis_index(name).astype(jnp.int32) for name in ALL)
 
-    t = tensor.transpose(0, 1, 3, 2)
-    parts = [core_cut(i * PAIRS, gz[None], t, species_factor.T, factor_three) for i in range(2)]
-    core = jnp.concatenate([own + swap(peer) for own, peer in parts], axis=2)
-    f2 = lax.dynamic_slice_in_dim(factor_two, gx * 16, 16)
-    f2 = jnp.broadcast_to(jnp.concatenate([f2[:8], f2[8:]], 1)[None], (64, 8, 128))
-    sent = jnp.concatenate([core.reshape(64, 128, 128), f2], 1)
+    t = pltpu.with_memory_space_constraint(tensor.transpose(0, 1, 3, 2), pltpu.HBM)
+    factors = jnp.concatenate([factor_three, jnp.pad(species_factor.T, ((0, 48), (0, 32)))], 1)
+    own_a, peer_a = core_cut(0, PAIRS[0], gz[None], t, factors)
+    own_b, peer_b = core_cut(*PAIRS, gz[None], t, factors)
+    sent = merge_first(gx[None], own_a, swap(peer_a), factor_two)
+    sent = merge_second(own_b, swap(peer_b), sent)
     c = to_all(sent, ("gx", "gy")).reshape(4, 16, 136, 128)
 
     e, gram = first_gram(c)

time: 183 us -> 170 us (0.929)
  Pallas kernels: 42.1 us -> 36.9 us
  other arithmetic: 5.74 us -> 0.93 us
  local copies, waits for them, and re-layouts: 4.1 us -> 0.63 us
    pallas_call x4 -> x6, Pallas kernels: 38 us -> 32.7 us  [the longest x2 17.7 us: core_cut(): pl.pallas_call(functools.partial(core_kernel, first, pairs), in_specs=[SM...]
    add x2 -> x0, other arithmetic: 4.75 us -> none  [per_device(): core = jnp.concatenate([own + swap(peer) for own, peer in parts], axis=2)]
    unnamed x9, local copies, waits for them, and re-layouts: 2.77 us -> 0.03 us
  transfers between devices with their start and end apart: 3 -> 3, of which waited for: 2 -> 2; matrix products, arithmetic and copies ran while one was open for 2% -> 0% of each run, Pallas kernels for 5% -> 5%
where the time goes in v2:
time: 170 us; the launch traced here: 169 us
  blocking collectives  113 us (66%)
  Pallas kernels  36.9 us (22%)
  waiting for transfers between devices  10.5 us (6%)
  starting transfers between devices  6.4 us (4%)
    all_to_all x4, blocking collectives, to_all(): return lax.all_to_all(x, names, 0, 0, tiled=True)  113 us
    pallas_call x2, Pallas kernels, core_cut(): pl.pallas_call(functools.partial(core_kernel, first, pairs), in_specs=[SM...  17.7 us
    all_to_all x1, waiting for transfers between devices, to_all(): return lax.all_to_all(x, names, 0, 0, tiled=True)  10.1 us
    pallas_call x1, Pallas kernels, second_image(): pl.pallas_call(second_kernel, in_specs=[VMEM, VMEM, HBM], out_specs=[VMEM...  7.55 us
    all_to_all x1, starting transfers between devices, to_all(): return lax.all_to_all(x, names, 0, 0, tiled=True)  4.65 us
    pallas_call x1, Pallas kernels, last_factor(): pl.pallas_call(last_kernel, in_specs=[SMEM, VMEM], out_specs=VMEM, out_sh...  3.76 us
  transfers between devices with their start and end apart: 3, of which 2 were waited for; matrix products, arithmetic and copies ran while one was open for 0% of the time, Pallas kernels for 5%

profile of v2, /device:TPU:1, one launch (start us, length us, event | category | flops | bytes accessed | tf_op | source)
XLA Modules:
  0.0 169.4 jit_solution(2746538860332759870)
XLA Ops:
  0.6 0.9 select_maximum_fusion.factors_ref
  1.5 12.1 %shard_map.69 = (f32[16,4,12,8,128]{4,3,2,1,0:T(8,128)}, f32[16,4,12,8,128]{4,3,2,1,0:T(8,128)}) custom-call(s32[1]{0:T(128)} %bitcast.gz_ref, f32[32,64,32,64]{3,2,1,0:T(8,128)} %bitcast.23, f32[64,128]{1,0:T(8,128)S(1)} %select_maximum_fusion.factors_ref), custom_call_target="tpu_custom_call" | custom-call | tf_op jit(solution)/shard_map/pallas_call | solution.py:138
  13.6 0.0 copy-start
  13.6 0.0 copy-start.2
  13.6 1.5 collective-permute-start.1
  15.1 5.6 %shard_map.68 = (f32[16,4,4,8,128]{4,3,2,1,0:T(8,128)}, f32[16,4,4,8,128]{4,3,2,1,0:T(8,128)}) custom-call(s32[1]{0:T(128)} %bitcast.gz_ref, f32[32,64,32,64]{3,2,1,0:T(8,128)} %bitcast.24, f32[64,128]{1,0:T(8,128)S(1)} %select_maximum_fusion.factors_ref), custom_call_target="tpu_custom_call" | custom-call | tf_op jit(solution)/shard_map/pallas_call | solution.py:138
  20.7 0.3 collective-permute-start
  21.0 0.0 collective-permute-done.1.other_ref
  21.0 0.0 copy-done
  21.0 0.0 copy-done.2
  21.0 0.0 copy-start.1
  21.0 2.4 %shard_map.70.sent_ref = f32[64,136,128]{2,1,0:T(8,128)S(1)} custom-call(s32[1]{0:T(128)} %bitcast.3.gx_ref, f32[16,4,12,8,128]{4,3,2,1,0:T(8,128)S(1)} %copy-done, f32[16,4,12,8,128]{4,3,2,1,0:T(8,128)} %collective-permute-done.1.other_ref, f32[64,64]{1,0:T(8,128)S(1)} %copy-done.2), custom_call_target="tpu_custom_call" | custom-call | tf_op jit(solution)/shard_map/pallas_call | solution.py:173
  23.4 0.4 collective-permute-done.other_ref
  23.8 0.0 copy-done.1
  23.8 1.3 shard_map.71
  25.2 65.9 %all_to_all.25 = f32[64,136,128]{2,1,0:T(8,128)S(1)} all-to-all(f32[64,136,128]{2,1,0:T(8,128)S(1)} %shard_map.71), channel_id=1, replica_groups=mesh['gx'=4,'gy'=16,'gz'=2] {'gx','gy'}, dimensions={0} | all-to-all | bytes 8912896 | tf_op jit(solution)/shard_map/all_to_all | solution.py:388
  91.1 0.0 copy-start.3
  91.1 3.0 %shard_map.72 = (f32[128,512]{1,0:T(8,128)S(1)}, f32[4,32,128]{2,1,0:T(8,128)S(1)}) custom-call(f32[4,16,136,128]{3,2,1,0:T(8,128)S(1)} %bitcast.16), custom_call_target="tpu_custom_call" | custom-call | tf_op jit(solution)/shard_map/pallas_call | solution.py:234
  94.1 17.7 %all_to_all.26 = f32[128,1,128]{2,1,0:T(1,128)S(1)} all-to-all(f32[128,1,128]{2,1,0:T(1,128)S(1)} %bitcast.22), channel_id=1, replica_groups=mesh['gx'=4,'gy'=16,'gz'=2] {'gx','gy','gz'}, dimensions={0} | all-to-all | bytes 131072 | tf_op jit(solution)/shard_map/all_to_all | solution.py:388
  111.8 0.0 copy-done.3
  111.8 0.3 shard_map.73
  112.1 14.5 %all_to_all.27 = f32[128,1,256]{2,1,0:T(1,128)S(1)} all-to-all(f32[128,1,256]{2,1,0:T(1,128)S(1)} %shard_map.73), channel_id=1, replica_groups=mesh['gx'=4,'gy'=16,'gz'=2] {'gx','gy','gz'}, dimensions={0} | all-to-all | bytes 262144 | tf_op jit(solution)/shard_map/all_to_all | solution.py:388
  126.6 7.6 %shard_map.74 = (f32[128,64]{1,0:T(8,128)S(1)}, f32[8,64,128]{2,1,0:T(8,128)S(1)}) custom-call(f32[128,256]{1,0:T(8,128)S(1)} %bitcast.19, f32[128,512]{1,0:T(8,128)S(1)} %get-tuple-element.15.e_ref, f32[4,16,136,128]{3,2,1,0:T(8,128)S(1)} %bitcast.17), custom_call_target="tpu_custom_call" | custom-call | tf_op jit(solution)/shard_map/pallas_call | solution.py:350
  134.2 15.1 %all_to_all.28.parts_ref = f32[128,4,128]{2,1,0:T(4,128)S(1)} all-to-all(f32[128,4,128]{2,1,0:T(4,128)S(1)} %bitcast.20), channel_id=1, replica_groups=mesh['gx'=4,'gy'=16,'gz'=2] {'gx','gy','gz'}, dimensions={0} | all-to-all | bytes 524288 | tf_op jit(solution)/shard_map/all_to_all | solution.py:388
  149.3 0.9 shard_map.75
  150.2 4.6 %all-to-all-start.4 = ((f32[128,4,128]{2,1,0:T(4,128)}), f32[128,4,128]{2,1,0:T(4,128)S(1)}, u32[]{:S(2)}, u32[]{:S(2)}) async-start(f32[128,4,128]{2,1,0:T(4,128)} %shard_map.75), calls=%async_computation.4 | async-start | bytes 524288 | tf_op jit(solution)/shard_map/all_to_all | solution.py:388
  154.8 0.1 pad_add_fusion.at_ref
  154.9 0.6 constant_dynamic-slice_fusion
  155.5 10.1 %all-to-all-done.4 = f32[128,4,128]{2,1,0:T(4,128)S(1)} async-done(((f32[128,4,128]{2,1,0:T(4,128)}), f32[128,4,128]{2,1,0:T(4,128)S(1)}, u32[]{:S(2)}, u32[]{:S(2)}) %all-to-all-start.4) | async-done | bytes 262176 | tf_op jit(solution)/shard_map/all_to_all | solution.py:388
  165.6 3.8 %shard_map.76 = f32[64,64]{1,0:T(8,128)} custom-call(s32[2]{0:T(128)S(1)} %pad_add_fusion.at_ref, f32[8,64,128]{2,1,0:T(8,128)S(1)} %bitcast.18), custom_call_target="tpu_custom_call" | custom-call | tf_op jit(solution)/shard_map/pallas_call | solution.py:378
  (1 shorter events, 0.0 us)
Async XLA Ops:
  13.6 7.4 %copy-start = (f32[16,4,12,8,128]{4,3,2,1,0:T(8,128)S(1)}, f32[16,4,12,8,128]{4,3,2,1,0:T(8,128)}, u32[]{:S(2)}) copy-start(f32[16,4,12,8,128]{4,3,2,1,0:T(8,128)} %get-tuple-element.12.own_ref) | copy-start | bytes 9437188
  13.6 7.4 %copy-start.2 = (f32[64,64]{1,0:T(8,128)S(1)}, f32[64,64]{1,0:T(8,128)}, u32[]{:S(2)}) copy-start(f32[64,64]{1,0:T(8,128)} %f2_ref.1) | copy-start | bytes 49156
  13.6 7.4 %collective-permute-start.1 = (f32[16,4,12,8,128]{4,3,2,1,0:T(8,128)}, f32[16,4,12,8,128]{4,3,2,1,0:T(8,128)}, u32[]{:S(2)}, u32[]{:S(2)}) collective-permute-start(f32[16,4,12,8,128]{4,3,2,1,0:T(8,128)} %get-tuple-element.13), channel_id=1, source_target_pairs={{0,1},{1,0},{2,3},{3,2},{4,5},{5,4},{6,7},{7,6},{8,9},{9,8},{10,11... | collective-permute-start | bytes 9437192 | tf_op jit(solution)/shard_map/ppermute | solution.py:392
  20.7 3.1 %collective-permute-start = (f32[16,4,4,8,128]{4,3,2,1,0:T(8,128)}, f32[16,4,4,8,128]{4,3,2,1,0:T(8,128)}, u32[]{:S(2)}, u32[]{:S(2)}) collective-permute-start(f32[16,4,4,8,128]{4,3,2,1,0:T(8,128)} %get-tuple-element.11), channel_id=1, source_target_pairs={{0,1},{1,0},{2,3},{3,2},{4,5},{5,4},{6,7},{7,6},{8,9},{9,8},{10,11... | collective-permute-start | bytes 3145736 | tf_op jit(solution)/shard_map/ppermute | solution.py:392
  21.0 2.8 %copy-start.1 = (f32[16,4,4,8,128]{4,3,2,1,0:T(8,128)S(1)}, f32[16,4,4,8,128]{4,3,2,1,0:T(8,128)}, u32[]{:S(2)}) copy-start(f32[16,4,4,8,128]{4,3,2,1,0:T(8,128)} %get-tuple-element.10.own_ref) | copy-start | bytes 3145732
  91.1 20.7 %copy-start.3 = (f32[32,64]{1,0:T(8,128)S(1)}, f32[32,64]{1,0:T(8,128)}, u32[]{:S(2)}) copy-start(f32[32,64]{1,0:T(8,128)} %f1_ref.1) | copy-start | bytes 24580
  150.2 15.4 %all-to-all-start.4 = ((f32[128,4,128]{2,1,0:T(4,128)}), f32[128,4,128]{2,1,0:T(4,128)S(1)}, u32[]{:S(2)}, u32[]{:S(2)}) async-start(f32[128,4,128]{2,1,0:T(4,128)} %shard_map.75), calls=%async_computation.4 | async-start | bytes 524288 | tf_op jit(solution)/shard_map/all_to_all | solution.py:388

commit v3 on v2

--- a/solution.py
+++ b/solution.py
@@ -65,16 +65,20 @@
 
 
 def core_kernel(
-    first, pairs, gz_ref, t_hbm, factors_ref, own_hbm, peer_hbm, own_ref, peer_ref, t_vmem, xa_ref, xb_ref, sems, out_sems
+    first, pairs, gz_ref, t_hbm, factors_ref, own_out, peer_hbm, *scratch
 ):
+    peer_ref, t_vmem, xa_ref, xb_ref, sems, out_sems = scratch[-6:]
+    own_ref = scratch[0] if len(scratch) > 6 else own_out
+
     def copy(i):
         slot = i % SLOTS
         return pltpu.make_async_copy(t_hbm.at[pl.ds(2 * (first + i), 2)], t_vmem.at[slot], sems.at[slot])
 
     def copies_out(i):
+        ends = [(peer_ref, peer_hbm)] + ([(own_ref, own_out)] if len(scratch) > 6 else [])
         return [
             pltpu.make_async_copy(ref.at[:, :, pl.ds(i, 2)], hbm.at[:, :, pl.ds(i, 2)], out_sems.at[k, i // 2])
-            for k, (ref, hbm) in enumerate(((own_ref, own_hbm), (peer_ref, peer_hbm)))
+            for k, (ref, hbm) in enumerate(ends)
         ]
 
     for i in range(min(SLOTS, pairs)):
@@ -134,15 +138,15 @@
 
 
 def core_cut(first, pairs, gz, tensor, factors):
-    part = pltpu.HBM((16, 4, pairs, 8, 128), F32)
+    shape = (16, 4, pairs, 8, 128)
+    stays = first == 0
     return pl.pallas_call(
         functools.partial(core_kernel, first, pairs),
         in_specs=[SMEM, HBM, VMEM],
-        out_specs=[HBM, HBM],
-        out_shape=[part, part],
-        scratch_shapes=[
-            pltpu.VMEM((16, 4, pairs, 8, 128), F32),
-            pltpu.VMEM((16, 4, pairs, 8, 128), F32),
+        out_specs=[VMEM if stays else HBM, HBM],
+        out_shape=[(pltpu.VMEM if stays else pltpu.HBM)(shape, F32), pltpu.HBM(shape, F32)],
+        scratch_shapes=[pltpu.VMEM(shape, F32)] * (1 if stays else 2)
+        + [
             pltpu.VMEM((SLOTS, 2, 64, 32, 64), F32),
             pltpu.VMEM((16, 64, 128), F32),
             pltpu.VMEM((16, 64, 128), F32),
@@ -191,15 +195,9 @@
 
 
 def first_kernel(c_ref, e_ref, gram_ref, fp_ref, g_ref):
-    step = pl.program_id(0)
-
-    @pl.when(step == 0)
-    def _():
-        fp_ref[...] = jnp.zeros_like(fp_ref)
-
     low = iota((8, 128), 1) < 64
-    total = fp_ref[...]
-    for y in range(4):
+    total = jnp.zeros((512, 256), F32)
+    for y in range(16):
         top, bottom = [], []
         for x in range(4):
             f2 = c_ref[x, y, 128:]
@@ -207,40 +205,31 @@
             top += [jnp.where(low, f2, 0.0), jnp.where(low, turned, 0.0)]
             bottom += [jnp.where(low, 0.0, turned), jnp.where(low, 0.0, f2)]
         w = wide(split(jnp.concatenate(top + bottom, 0)))
-        total += mm_wide(c_ref[:, y, :128].reshape(512, 128), w)
-    fp_ref[...] = total
-
-    @pl.when(step == pl.num_programs(0) - 1)
-    def _():
-        gram, cross = jnp.zeros((128, 128), F32), jnp.zeros((128, 128), F32)
-        for r in range(4):
-            e = fp_ref[pl.ds(r, 128, stride=4), :]
-            e_ref[:, r * 128 : (r + 1) * 128] = e
-            eh, el = split(e)
-            gram += mm(eh, eh, NT)
-            cross += mm(eh, el, NT)
-        g_ref[...] = gram + (cross + cross.T)
-        group = iota((32, 128), 1) // 32
-        rows = [g_ref[pl.ds(i, 32, stride=4), :] for i in range(4)]
-        for x in range(4):
-            block = jnp.zeros((32, 128), F32)
-            for i in range(4):
-                moved = pltpu.roll(rows[i], 32 * ((i - x) % 4), 1) if i != x else rows[i]
-                block = jnp.where(group == i, moved, block)
-            gram_ref[x] = block
+        total += mm(jnp.concatenate(split(c_ref[:, y, :128].reshape(512, 128)), 1), w, NN)
+    fp_ref[...] = total[:, :128] + total[:, 128:]
+    gram, cross = jnp.zeros((128, 128), F32), jnp.zeros((128, 128), F32)
+    for r in range(4):
+        e = fp_ref[pl.ds(r, 128, stride=4), :]
+        e_ref[:, r * 128 : (r + 1) * 128] = e
+        eh, el = split(e)
+        gram += mm(eh, eh, NT)
+        cross += mm(eh, el, NT)
+    g_ref[...] = gram + (cross + cross.T)
+    group = iota((32, 128), 1) >> 5
+    rows = [g_ref[pl.ds(i, 32, stride=4), :] for i in range(4)]
+    for x in range(4):
+        block = jnp.zeros((32, 128), F32)
+        for i in range(4):
+            moved = pltpu.roll(rows[i], 32 * ((i - x) % 4), 1) if i != x else rows[i]
+            block = jnp.where(group == i, moved, block)
+        gram_ref[x] = block
 
 
 def first_gram(c):
     return pl.pallas_call(
         first_kernel,
-        grid=(4,),
-        in_specs=[
-            pl.BlockSpec((4, 4, 136, 128), lambda i: (0, i, 0, 0)),
-        ],
-        out_specs=[
-            pl.BlockSpec((128, 512), lambda i: (0, 0)),
-            pl.BlockSpec((4, 32, 128), lambda i: (0, 0, 0)),
-        ],
+        in_specs=[VMEM],
+        out_specs=[VMEM, VMEM],
         out_shape=[jax.ShapeDtypeStruct((128, 512), F32), jax.ShapeDtypeStruct((4, 32, 128), F32)],
         scratch_shapes=[pltpu.VMEM((512, 128), F32), pltpu.VMEM((128, 128), F32)],
         compiler_params=PARAMS,
@@ -315,7 +304,7 @@
     return m[:, 64:] * lax.rsqrt(diagonal)
 
 
-def second_kernel(parts_ref, e_ref, c_ref, new_ref, part_ref, i_ref, y_ref, c_vmem, sem):
+def second_kernel(gx_ref, parts_ref, e_ref, c_ref, new_ref, part_ref, i_ref, y_ref, c_vmem, sem):
     copy = pltpu.make_async_copy(c_ref.at[:, :, pl.ds(0, 128)], c_vmem, sem)
     copy.start()
     rows = jnp.sum(parts_ref[...].reshape(4, 32, 256), axis=0)
@@ -326,32 +315,34 @@
     projected = split(mm_f32(image, e_ref[...], TN))
     inverse = split(inverse_factor(normal))
     basis = mm3(split(image), inverse, NT)
-    new_ref[...] = basis * math.sqrt(128)
+    i_ref[...] = basis * math.sqrt(128)
+    new_ref[...] = i_ref[pl.ds(pl.multiple_of(32 * gx_ref[0], 32), 32), :]
     y = mm_f32(basis, mm3(inverse, projected, NN), NN)
     for r in range(4):
         y_ref[pl.ds(r, 128, stride=4), :] = y[:, r * 128 : (r + 1) * 128]
     yt = split(y_ref[...].T)
+    both = jnp.concatenate(yt, 0)
     low = iota((64, 128), 1) < 64
     copy.wait()
 
-    def both(i, _):
-        halves = []
-        for k in range(2):
-            c = split(c_vmem[:, 2 * i + k].reshape(512, 128))
-            o = mm3(yt, c, NN)
-            halves.append(o[:64, :] + pltpu.roll(o[64:, :], 64, 1))
+    def two(i, _):
+        c = [c_vmem[:, 2 * i + k].reshape(512, 128) for k in range(2)]
+        ch, cl = split(jnp.concatenate(c, 1))
+        o = mm(both, ch, NN)
+        o = o[:128] + o[128:] + mm(yt[0], cl, NN)
+        halves = [o[:64, at : at + 128] + pltpu.roll(o[64:, at : at + 128], 64, 1) for at in (0, 128)]
         part_ref[i] = jnp.where(low, halves[0], pltpu.roll(halves[1], 64, 1))
         return 0
 
-    lax.fori_loop(0, 8, both, 0)
-
-
-def second_image(parts, e, c):
+    lax.fori_loop(0, 8, two, 0, unroll=True)
+
+
+def second_image(gx, parts, e, c):
     return pl.pallas_call(
         second_kernel,
-        in_specs=[VMEM, VMEM, HBM],
+        in_specs=[SMEM, VMEM, VMEM, HBM],
         out_specs=[VMEM, VMEM],
-        out_shape=[jax.ShapeDtypeStruct((128, 64), F32), jax.ShapeDtypeStruct((8, 64, 128), F32)],
+        out_shape=[jax.ShapeDtypeStruct((32, 64), F32), jax.ShapeDtypeStruct((8, 64, 128), F32)],
         scratch_shapes=[
             pltpu.VMEM((128, 64), F32),
             pltpu.VMEM((512, 128), F32),
@@ -359,7 +350,7 @@
             pltpu.SemaphoreType.DMA,
         ],
         compiler_params=PARAMS,
-    )(parts, e, c)
+    )(gx, parts, e, c)
 
 
 def last_kernel(at_ref, image_ref, new_ref):
@@ -388,6 +379,10 @@
     return lax.all_to_all(x, names, 0, 0, tiled=True)
 
 
+def in_hbm(x):
+    return pltpu.with_memory_space_constraint(x, pltpu.HBM)
+
+
 def swap(x):
     return lax.ppermute(x, "gz", [(0, 1), (1, 0)])
 
@@ -395,7 +390,7 @@
 def per_device(tensor, factor_one, factor_two, factor_three, species_factor):
     gx, gy, gz = (lax.axis_index(name).astype(jnp.int32) for name in ALL)
 
-    t = pltpu.with_memory_space_constraint(tensor.transpose(0, 1, 3, 2), pltpu.HBM)
+    t = in_hbm(tensor.transpose(0, 1, 3, 2))
     factors = jnp.concatenate([factor_three, jnp.pad(species_factor.T, ((0, 48), (0, 32)))], 1)
     own_a, peer_a = core_cut(0, PAIRS[0], gz[None], t, factors)
     own_b, peer_b = core_cut(*PAIRS, gz[None], t, factors)
@@ -405,10 +400,10 @@
 
     e, gram = first_gram(c)
     rows = image_rows(to_all(gram.reshape(128, 1, 128)).reshape(128, 128), factor_one)
-    new_one, second_part = second_image(to_all(rows).reshape(128, 256), e, c)
+    new_one, second_part = second_image(gx[None], to_all(rows).reshape(128, 256), e, c)
     second = to_all(sum_for_all(to_all(second_part.reshape(128, 4, 128)))).reshape(8, 64, 128)
     new_two = last_factor(jnp.stack([gy // 2, gy % 2]), second)
-    return lax.dynamic_slice_in_dim(new_one, gx * 32, 32), new_two
+    return new_one, new_two
 
 
 def solution(mesh):

time: 170 us -> 165 us (0.971)
  Pallas kernels: 36.9 us -> 32.5 us
    pallas_call x2, Pallas kernels: 10.5 us -> 6.82 us  [the longest x1 4.73 us: second_image(): pl.pallas_call(second_kernel, in_specs=[SMEM, VMEM, VMEM, HBM], out_specs...]
where the time goes in v3:
time: 165 us
  blocking collectives  113 us (68%)
  Pallas kernels  32.5 us (20%)
  waiting for transfers between devices  11.3 us (7%)
  starting transfers between devices  6.24 us (4%)
    all_to_all x4, blocking collectives, to_all(): return lax.all_to_all(x, names, 0, 0, tiled=True)  113 us
    pallas_call x2, Pallas kernels, core_cut(): pl.pallas_call(functools.partial(core_kernel, first, pairs), in_specs=[SM...  17 us
    all_to_all x1, waiting for transfers between devices, to_all(): return lax.all_to_all(x, names, 0, 0, tiled=True)  10.7 us
    pallas_call x1, Pallas kernels, second_image(): pl.pallas_call(second_kernel, in_specs=[SMEM, VMEM, VMEM, HBM], out_specs...  4.73 us
    all_to_all x1, starting transfers between devices, to_all(): return lax.all_to_all(x, names, 0, 0, tiled=True)  4.65 us
    pallas_call x1, Pallas kernels, last_factor(): pl.pallas_call(last_kernel, in_specs=[SMEM, VMEM], out_specs=VMEM, out_sh...  3.76 us
  transfers between devices with their start and end apart: 3, of which 2 were waited for; matrix products, arithmetic and copies ran while one was open for 0% of the time, Pallas kernels for 5%

profile of v3, /device:TPU:1, one launch (start us, length us, event | category | flops | bytes accessed | tf_op | source)
XLA Modules:
  0.0 164.8 jit_solution(4935006820132001389)
XLA Ops:
  0.6 0.9 select_maximum_fusion.factors_ref
  1.5 11.3 %shard_map.69 = (f32[16,4,12,8,128]{4,3,2,1,0:T(8,128)S(1)}, f32[16,4,12,8,128]{4,3,2,1,0:T(8,128)}) custom-call(s32[1]{0:T(128)} %bitcast.1.gz_ref, f32[32,64,32,64]{3,2,1,0:T(8,128)} %bitcast.23, f32[64,128]{1,0:T(8,128)S(1)} %select_maximum_fusion.factors_ref), custom_call_target="tpu_custom_call" | custom-call | tf_op jit(solution)/shard_map/pallas_call | solution.py:143
  12.8 0.0 copy-start.1
  12.8 1.5 collective-permute-start.1
  14.3 5.7 %shard_map.68 = (f32[16,4,4,8,128]{4,3,2,1,0:T(8,128)}, f32[16,4,4,8,128]{4,3,2,1,0:T(8,128)}) custom-call(s32[1]{0:T(128)} %bitcast.1.gz_ref, f32[32,64,32,64]{3,2,1,0:T(8,128)} %bitcast.24, f32[64,128]{1,0:T(8,128)S(1)} %select_maximum_fusion.factors_ref), custom_call_target="tpu_custom_call" | custom-call | tf_op jit(solution)/shard_map/pallas_call | solution.py:143
  20.0 0.1 collective-permute-start
  20.1 0.0 collective-permute-done.1.other_ref
  20.1 0.0 copy-done.1
  20.1 0.0 copy-start
  20.1 2.4 %shard_map.70.sent_ref = f32[64,136,128]{2,1,0:T(8,128)S(1)} custom-call(s32[1]{0:T(128)} %bitcast.gx_ref, f32[16,4,12,8,128]{4,3,2,1,0:T(8,128)S(1)} %get-tuple-element.12.own_ref, f32[16,4,12,8,128]{4,3,2,1,0:T(8,128)} %collective-permute-done.1.other_ref, f32[64,64]{1,0:T(8,128)S(1)} %copy-done.1), custom_call_target="tpu_custom_call" | custom-call | tf_op jit(solution)/shard_map/pallas_call | solution.py:177
  22.5 0.6 collective-permute-done.other_ref
  23.1 0.0 copy-done
  23.1 1.3 shard_map.71
  24.4 65.8 %all_to_all.25 = f32[64,136,128]{2,1,0:T(8,128)S(1)} all-to-all(f32[64,136,128]{2,1,0:T(8,128)S(1)} %shard_map.71), channel_id=1, replica_groups=mesh['gx'=4,'gy'=16,'gz'=2] {'gx','gy'}, dimensions={0} | all-to-all | bytes 8912896 | tf_op jit(solution)/shard_map/all_to_all | solution.py:379
  90.3 0.0 copy-start.2
  90.3 2.1 %shard_map.72 = (f32[128,512]{1,0:T(8,128)S(1)}, f32[4,32,128]{2,1,0:T(8,128)S(1)}) custom-call(f32[4,16,136,128]{3,2,1,0:T(8,128)S(1)} %bitcast.16), custom_call_target="tpu_custom_call" | custom-call | tf_op jit(solution)/shard_map/pallas_call | solution.py:229
  92.4 17.7 %all_to_all.26 = f32[128,1,128]{2,1,0:T(1,128)S(1)} all-to-all(f32[128,1,128]{2,1,0:T(1,128)S(1)} %bitcast.22), channel_id=1, replica_groups=mesh['gx'=4,'gy'=16,'gz'=2] {'gx','gy','gz'}, dimensions={0} | all-to-all | bytes 131072 | tf_op jit(solution)/shard_map/all_to_all | solution.py:379
  110.1 0.0 copy-done.2
  110.1 0.3 shard_map.73
  110.4 14.5 %all_to_all.27 = f32[128,1,256]{2,1,0:T(1,128)S(1)} all-to-all(f32[128,1,256]{2,1,0:T(1,128)S(1)} %shard_map.73), channel_id=1, replica_groups=mesh['gx'=4,'gy'=16,'gz'=2] {'gx','gy','gz'}, dimensions={0} | all-to-all | bytes 262144 | tf_op jit(solution)/shard_map/all_to_all | solution.py:379
  124.9 4.7 %shard_map.74 = (f32[32,64]{1,0:T(8,128)}, f32[8,64,128]{2,1,0:T(8,128)S(1)}) custom-call(s32[1]{0:T(128)} %bitcast.gx_ref, f32[128,256]{1,0:T(8,128)S(1)} %bitcast.19, f32[128,512]{1,0:T(8,128)S(1)} %get-tuple-element.15.e_ref, f32[4,16,136,128]{3,2,1,0:T(8,128)S(1)} %bitcast.17), custom_call_target="tpu_custom_call" | custom-call | tf_op jit(solution)/shard_map/pallas_call | solution.py:341
  129.6 15.1 %all_to_all.28.parts_ref = f32[128,4,128]{2,1,0:T(4,128)S(1)} all-to-all(f32[128,4,128]{2,1,0:T(4,128)S(1)} %bitcast.20), channel_id=1, replica_groups=mesh['gx'=4,'gy'=16,'gz'=2] {'gx','gy','gz'}, dimensions={0} | all-to-all | bytes 524288 | tf_op jit(solution)/shard_map/all_to_all | solution.py:379
  144.7 0.9 shard_map.75
  145.6 4.6 %all-to-all-start.4 = ((f32[128,4,128]{2,1,0:T(4,128)}), f32[128,4,128]{2,1,0:T(4,128)S(1)}, u32[]{:S(2)}, u32[]{:S(2)}) async-start(f32[128,4,128]{2,1,0:T(4,128)} %shard_map.75), calls=%async_computation.4 | async-start | bytes 524288 | tf_op jit(solution)/shard_map/all_to_all | solution.py:379
  150.3 0.1 pad_add_fusion.at_ref
  150.4 10.7 %all-to-all-done.4 = f32[128,4,128]{2,1,0:T(4,128)S(1)} async-done(((f32[128,4,128]{2,1,0:T(4,128)}), f32[128,4,128]{2,1,0:T(4,128)S(1)}, u32[]{:S(2)}, u32[]{:S(2)}) %all-to-all-start.4) | async-done | bytes 262176 | tf_op jit(solution)/shard_map/all_to_all | solution.py:379
  161.1 3.8 %shard_map.76 = f32[64,64]{1,0:T(8,128)} custom-call(s32[2]{0:T(128)S(1)} %pad_add_fusion.at_ref, f32[8,64,128]{2,1,0:T(8,128)S(1)} %bitcast.18), custom_call_target="tpu_custom_call" | custom-call | tf_op jit(solution)/shard_map/pallas_call | solution.py:369
  (1 shorter events, 0.0 us)
Async XLA Ops:
  12.8 7.3 %copy-start.1 = (f32[64,64]{1,0:T(8,128)S(1)}, f32[64,64]{1,0:T(8,128)}, u32[]{:S(2)}) copy-start(f32[64,64]{1,0:T(8,128)} %f2_ref.1) | copy-start | bytes 49156
  12.8 7.3 %collective-permute-start.1 = (f32[16,4,12,8,128]{4,3,2,1,0:T(8,128)}, f32[16,4,12,8,128]{4,3,2,1,0:T(8,128)}, u32[]{:S(2)}, u32[]{:S(2)}) collective-permute-start(f32[16,4,12,8,128]{4,3,2,1,0:T(8,128)} %get-tuple-element.13), channel_id=1, source_target_pairs={{0,1},{1,0},{2,3},{3,2},{4,5},{5,4},{6,7},{7,6},{8,9},{9,8},{10,11... | collective-permute-start | bytes 9437192 | tf_op jit(solution)/shard_map/ppermute | solution.py:387
  20.0 3.1 %collective-permute-start = (f32[16,4,4,8,128]{4,3,2,1,0:T(8,128)}, f32[16,4,4,8,128]{4,3,2,1,0:T(8,128)}, u32[]{:S(2)}, u32[]{:S(2)}) collective-permute-start(f32[16,4,4,8,128]{4,3,2,1,0:T(8,128)} %get-tuple-element.11), channel_id=1, source_target_pairs={{0,1},{1,0},{2,3},{3,2},{4,5},{5,4},{6,7},{7,6},{8,9},{9,8},{10,11... | collective-permute-start | bytes 3145736 | tf_op jit(solution)/shard_map/ppermute | solution.py:387
  20.1 3.0 %copy-start = (f32[16,4,4,8,128]{4,3,2,1,0:T(8,128)S(1)}, f32[16,4,4,8,128]{4,3,2,1,0:T(8,128)}, u32[]{:S(2)}) copy-start(f32[16,4,4,8,128]{4,3,2,1,0:T(8,128)} %get-tuple-element.10.own_ref) | copy-start | bytes 3145732
  90.3 19.8 %copy-start.2 = (f32[32,64]{1,0:T(8,128)S(1)}, f32[32,64]{1,0:T(8,128)}, u32[]{:S(2)}) copy-start(f32[32,64]{1,0:T(8,128)} %f1_ref.1) | copy-start | bytes 24580
  145.6 15.4 %all-to-all-start.4 = ((f32[128,4,128]{2,1,0:T(4,128)}), f32[128,4,128]{2,1,0:T(4,128)S(1)}, u32[]{:S(2)}, u32[]{:S(2)}) async-start(f32[128,4,128]{2,1,0:T(4,128)} %shard_map.75), calls=%async_computation.4 | async-start | bytes 524288 | tf_op jit(solution)/shard_map/all_to_all | solution.py:379

commit v4 on v3

--- a/solution.py
+++ b/solution.py
@@ -17,7 +17,7 @@
 SLOTS = 6
 VMEM = pl.BlockSpec(memory_space=pltpu.VMEM)
 PARAMS = pltpu.CompilerParams(vmem_limit_bytes=12 << 20)
-LARGE = pltpu.CompilerParams(vmem_limit_bytes=24 << 20)
+LARGE = pltpu.CompilerParams(vmem_limit_bytes=28 << 20)
 HBM = pl.BlockSpec(memory_space=pltpu.HBM)
 SMEM = pl.BlockSpec(memory_space=pltpu.SMEM)
 
@@ -64,24 +64,31 @@
     )
 
 
-def core_kernel(
-    first, pairs, gz_ref, t_hbm, factors_ref, own_out, peer_hbm, *scratch
-):
-    peer_ref, t_vmem, xa_ref, xb_ref, sems, out_sems = scratch[-6:]
-    own_ref = scratch[0] if len(scratch) > 6 else own_out
+def core_kernel(chunk, gz_ref, t_hbm, factors_ref, *rest):
+    first, pairs = (0, PAIRS[0]) if chunk == 0 else PAIRS
+    if chunk == 0:
+        own_out, peer_hbm, ready_ref, *scratch = rest
+        own_ref = own_out
+    else:
+        ready_ref, own_out, peer_hbm, own_ref, *scratch = rest
+    peer_ref, t_vmem, xa_ref, xb_ref, sems, out_sems, ready_sem = scratch
+    skip = 2 * chunk
 
     def copy(i):
         slot = i % SLOTS
         return pltpu.make_async_copy(t_hbm.at[pl.ds(2 * (first + i), 2)], t_vmem.at[slot], sems.at[slot])
 
+    def copy_ready():
+        return pltpu.make_async_copy(t_hbm.at[pl.ds(2 * PAIRS[0], 4)], ready_ref, ready_sem)
+
     def copies_out(i):
-        ends = [(peer_ref, peer_hbm)] + ([(own_ref, own_out)] if len(scratch) > 6 else [])
+        ends = [(peer_ref, peer_hbm)] + ([(own_ref, own_out)] if chunk == 1 else [])
         return [
             pltpu.make_async_copy(ref.at[:, :, pl.ds(i, 2)], hbm.at[:, :, pl.ds(i, 2)], out_sems.at[k, i // 2])
             for k, (ref, hbm) in enumerate(ends)
         ]
 
-    for i in range(min(SLOTS, pairs)):
+    for i in range(skip, min(SLOTS, pairs)):
         copy(i).start()
 
     q = ((iota((128, 16), 0) >> 3) + 8 * gz_ref[0]) & 15
@@ -95,11 +102,10 @@
     same = (iota((128, 128), 0) >> 6) == ((iota((128, 128), 1) >> 2) & 1)
     w3 = wide(spread(rows, factors_ref[:, :64], columns, same))
 
-    def contract_s(i, xs_ref):
+    def contract_s(t_ref, xs_ref):
         for g in range(8):
             at = slice(g * 8, g * 8 + 8)
-            t = [t_vmem[i % SLOTS, a, at].reshape(256, 64) for a in range(2)]
-            th, tl = split(jnp.concatenate(t, 1))
+            th, tl = split(jnp.concatenate([t_ref[a, at].reshape(256, 64) for a in range(2)], 1))
             y = mm(sf[0], jnp.concatenate([th, tl], 1), NN)
             x = y[:, :128] + y[:, 128:] + mm(sf[1], th, NN)
             xs_ref[:, at, :] = x.reshape(16, 8, 128)
@@ -113,57 +119,86 @@
             else:
                 peer_ref[:, k - 4, i] = o
 
-    def two_pairs(step, _):
-        i = 2 * step
-        copy(i).wait()
-        contract_s(i, xa_ref)
-        copy(i + 1).wait()
-        contract_s(i + 1, xb_ref)
+    def finish(i):
         contract_c(i, xa_ref)
         contract_c(i + 1, xb_ref)
         for out in copies_out(i):
             out.start()
 
+    def two_pairs(step, _):
+        i = 2 * step
+        copy(i).wait()
+        contract_s(t_vmem.at[i % SLOTS], xa_ref)
+        copy(i + 1).wait()
+        contract_s(t_vmem.at[(i + 1) % SLOTS], xb_ref)
+        finish(i)
+
         @pl.when(i + SLOTS < pairs)
         def _():
             copy(i + SLOTS).start()
             copy(i + SLOTS + 1).start()
 
+        if chunk == 0:
+
+            @pl.when(i + SLOTS == pairs)
+            def _():
+                copy_ready().start()
+
         return 0
 
-    lax.fori_loop(0, pairs // 2, two_pairs, 0)
+    if chunk == 1:
+        contract_s(ready_ref.at[pl.ds(0, 2)], xa_ref)
+        contract_s(ready_ref.at[pl.ds(2, 2)], xb_ref)
+        finish(0)
+    lax.fori_loop(chunk, pairs // 2, two_pairs, 0)
     for i in range(0, pairs, 2):
         for out in copies_out(i):
             out.wait()
-
-
-def core_cut(first, pairs, gz, tensor, factors):
-    shape = (16, 4, pairs, 8, 128)
-    stays = first == 0
-    return pl.pallas_call(
-        functools.partial(core_kernel, first, pairs),
-        in_specs=[SMEM, HBM, VMEM],
-        out_specs=[VMEM if stays else HBM, HBM],
-        out_shape=[(pltpu.VMEM if stays else pltpu.HBM)(shape, F32), pltpu.HBM(shape, F32)],
-        scratch_shapes=[pltpu.VMEM(shape, F32)] * (1 if stays else 2)
+    if chunk == 0:
+        copy_ready().wait()
+
+
+def core_cut(chunk, gz, tensor, factors, *ready):
+    pairs = PAIRS[chunk]
+    shape, fetched = (16, 4, pairs, 8, 128), (4, 64, 32, 64)
+    peer = pltpu.HBM(shape, F32)
+    if chunk == 0:
+        out_specs, out_shape = [VMEM, HBM, VMEM], [pltpu.VMEM(shape, F32), peer, pltpu.VMEM(fetched, F32)]
+    else:
+        out_specs, out_shape = [HBM, HBM], [peer, peer]
+    return pl.pallas_call(
+        functools.partial(core_kernel, chunk),
+        in_specs=[SMEM, HBM, VMEM] + [VMEM] * chunk,
+        out_specs=out_specs,
+        out_shape=out_shape,
+        scratch_shapes=[pltpu.VMEM(shape, F32)] * (1 + chunk)
         + [
             pltpu.VMEM((SLOTS, 2, 64, 32, 64), F32),
             pltpu.VMEM((16, 64, 128), F32),
             pltpu.VMEM((16, 64, 128), F32),
             pltpu.SemaphoreType.DMA((SLOTS,)),
             pltpu.SemaphoreType.DMA((2, pairs // 2)),
+            pltpu.SemaphoreType.DMA,
         ],
         compiler_params=LARGE,
-    )(gz, tensor, factors)
-
-
-def merge_first_kernel(gx_ref, own_ref, other_ref, f2_ref, out_ref):
+    )(gz, tensor, factors, *ready)
+
+
+def merge_first_kernel(gx_ref, own_ref, other_hbm, f2_ref, out_ref, other_ref, sems):
     rows = 8 * PAIRS[0]
-    for g in range(16):
-        out_ref[4 * g : 4 * g + 4, :rows] = (own_ref[g] + other_ref[g]).reshape(4, rows, 128)
+    copies = [
+        pltpu.make_async_copy(other_hbm.at[pl.ds(2 * g, 2)], other_ref.at[pl.ds(2 * g, 2)], sems.at[g])
+        for g in range(8)
+    ]
+    for copy in copies:
+        copy.start()
     f2 = f2_ref[pl.ds(pl.multiple_of(16 * gx_ref[0], 16), 16), :]
     f2 = jnp.concatenate([f2[:8], f2[8:]], 1)
     out_ref[:, 128:] = jnp.broadcast_to(f2[None], (64, 8, 128))
+    for g in range(16):
+        if g % 2 == 0:
+            copies[g // 2].wait()
+        out_ref[4 * g : 4 * g + 4, :rows] = (own_ref[g] + other_ref[g]).reshape(4, rows, 128)
 
 
 def merge_second_kernel(own_ref, other_ref, sent_ref, out_ref):
@@ -176,11 +211,12 @@
 def merge_first(gx, own, other, f2):
     return pl.pallas_call(
         merge_first_kernel,
-        in_specs=[SMEM, VMEM, VMEM, VMEM],
+        in_specs=[SMEM, VMEM, HBM, VMEM],
         out_specs=VMEM,
         out_shape=pltpu.VMEM((64, 136, 128), F32),
-        compiler_params=PARAMS,
-    )(gx, own, other, f2)
+        scratch_shapes=[pltpu.VMEM(own.shape, F32), pltpu.SemaphoreType.DMA((8,))],
+        compiler_params=PARAMS,
+    )(gx, own, in_hbm(other), f2)
 
 
 def merge_second(own, other, sent):
@@ -392,8 +428,8 @@
 
     t = in_hbm(tensor.transpose(0, 1, 3, 2))
     factors = jnp.concatenate([factor_three, jnp.pad(species_factor.T, ((0, 48), (0, 32)))], 1)
-    own_a, peer_a = core_cut(0, PAIRS[0], gz[None], t, factors)
-    own_b, peer_b = core_cut(*PAIRS, gz[None], t, factors)
+    own_a, peer_a, ready = core_cut(0, gz[None], t, factors)
+    own_b, peer_b = core_cut(1, gz[None], t, factors, ready)
     sent = merge_first(gx[None], own_a, swap(peer_a), factor_two)
     sent = merge_second(own_b, swap(peer_b), sent)
     c = to_all(sent, ("gx", "gy")).reshape(4, 16, 136, 128)

time: 165 us -> 163 us (0.988)
  Pallas kernels: 32.5 us -> 30.7 us
    pallas_call x3, Pallas kernels: 19.4 us -> 17.5 us  [the longest x2 15.5 us: core_cut(): pl.pallas_call(functools.partial(core_kernel, chunk), in_specs=[SMEM, HBM...]
  transfers between devices with their start and end apart: 3 -> 3, of which waited for: 2 -> 2; matrix products, arithmetic and copies ran while one was open for 0% -> 0% of each run, Pallas kernels for 5% -> 4%
where the time goes in v4:
time: 163 us
  blocking collectives  112 us (69%)
  Pallas kernels  30.7 us (19%)
  waiting for transfers between devices  12 us (7%)
  starting transfers between devices  6.25 us (4%)
    all_to_all x4, blocking collectives, to_all(): return lax.all_to_all(x, names, 0, 0, tiled=True)  112 us
    pallas_call x2, Pallas kernels, core_cut(): pl.pallas_call(functools.partial(core_kernel, chunk), in_specs=[SMEM, HBM...  15.5 us
    all_to_all x1, waiting for transfers between devices, to_all(): return lax.all_to_all(x, names, 0, 0, tiled=True)  10.7 us
    pallas_call x1, Pallas kernels, second_image(): pl.pallas_call(second_kernel, in_specs=[SMEM, VMEM, VMEM, HBM], out_specs...  4.73 us
    all_to_all x1, starting transfers between devices, to_all(): return lax.all_to_all(x, names, 0, 0, tiled=True)  4.65 us
    pallas_call x1, Pallas kernels, last_factor(): pl.pallas_call(last_kernel, in_specs=[SMEM, VMEM], out_specs=VMEM, out_sh...  3.76 us
  transfers between devices with their start and end apart: 3, of which 2 were waited for; matrix products, arithmetic and copies ran while one was open for 0% of the time, Pallas kernels for 4%

profile of v4, /device:TPU:1, one launch (start us, length us, event | category | flops | bytes accessed | tf_op | source)
XLA Modules:
  0.0 163.1 jit_solution(430824866646097352)
XLA Ops:
  0.6 0.9 select_maximum_fusion.factors_ref
  1.5 11.3 %shard_map.68 = (f32[16,4,12,8,128]{4,3,2,1,0:T(8,128)S(1)}, f32[16,4,12,8,128]{4,3,2,1,0:T(8,128)}, f32[4,64,32,64]{3,2,1,0:T(8,128)S(1)}) custom-call(s32[1]{0:T(128)} %bitcast.1.gz_ref, f32[32,64,32,64]{3,2,1,0:T(8,128)} %bitcast.23, f32[64,128]{1,0:T(8,128)S(1)} %select_maximum_fusion.factors_ref), custom_call_target="tpu_custom_call" | custom-call | tf_op jit(solution)/shard_map/pallas_call | solution.py:169
  12.8 1.5 collective-permute-start.1
  14.3 0.0 copy-start.1
  14.3 4.2 %shard_map.69 = (f32[16,4,4,8,128]{4,3,2,1,0:T(8,128)}, f32[16,4,4,8,128]{4,3,2,1,0:T(8,128)}) custom-call(s32[1]{0:T(128)} %bitcast.1.gz_ref, f32[32,64,32,64]{3,2,1,0:T(8,128)} %bitcast.24, f32[64,128]{1,0:T(8,128)S(1)} %select_maximum_fusion.factors_ref, f32[4,64,32,64]{3,2,1,0:T(8,128)S(1)} %get-tuple-element.11.rest_0_), custom_call_target="tpu_custom_call" | custom-call | tf_op jit(solution)/shard_map/pallas_call | solution.py:169
  18.5 0.1 collective-permute-start
  18.6 1.3 collective-permute-done.1.other_hbm
  19.9 0.0 copy-done.1
  19.9 0.0 copy-start
  19.9 2.0 %shard_map.70.sent_ref = f32[64,136,128]{2,1,0:T(8,128)S(1)} custom-call(s32[1]{0:T(128)} %bitcast.gx_ref, f32[16,4,12,8,128]{4,3,2,1,0:T(8,128)S(1)} %get-tuple-element.14.own_ref, f32[16,4,12,8,128]{4,3,2,1,0:T(8,128)} %collective-permute-done.1.other_hbm, f32[64,64]{1,0:T(8,128)S(1)} %copy-done.1), custom_call_target="tpu_custom_call" | custom-call | tf_op jit(solution)/shard_map/pallas_call | solution.py:212
  22.0 0.0 collective-permute-done.other_ref
  22.0 0.1 copy-done
  22.1 1.3 shard_map.71
  23.4 65.5 %all_to_all.25 = f32[64,136,128]{2,1,0:T(8,128)S(1)} all-to-all(f32[64,136,128]{2,1,0:T(8,128)S(1)} %shard_map.71), channel_id=1, replica_groups=mesh['gx'=4,'gy'=16,'gz'=2] {'gx','gy'}, dimensions={0} | all-to-all | bytes 8912896 | tf_op jit(solution)/shard_map/all_to_all | solution.py:415
  89.0 0.0 copy-start.2
  89.0 2.1 %shard_map.72 = (f32[128,512]{1,0:T(8,128)S(1)}, f32[4,32,128]{2,1,0:T(8,128)S(1)}) custom-call(f32[4,16,136,128]{3,2,1,0:T(8,128)S(1)} %bitcast.16), custom_call_target="tpu_custom_call" | custom-call | tf_op jit(solution)/shard_map/pallas_call | solution.py:265
  91.0 17.3 %all_to_all.26 = f32[128,1,128]{2,1,0:T(1,128)S(1)} all-to-all(f32[128,1,128]{2,1,0:T(1,128)S(1)} %bitcast.22), channel_id=1, replica_groups=mesh['gx'=4,'gy'=16,'gz'=2] {'gx','gy','gz'}, dimensions={0} | all-to-all | bytes 131072 | tf_op jit(solution)/shard_map/all_to_all | solution.py:415
  108.3 0.0 copy-done.2
  108.3 0.3 shard_map.73
  108.6 14.5 %all_to_all.27 = f32[128,1,256]{2,1,0:T(1,128)S(1)} all-to-all(f32[128,1,256]{2,1,0:T(1,128)S(1)} %shard_map.73), channel_id=1, replica_groups=mesh['gx'=4,'gy'=16,'gz'=2] {'gx','gy','gz'}, dimensions={0} | all-to-all | bytes 262144 | tf_op jit(solution)/shard_map/all_to_all | solution.py:415
  123.1 4.7 %shard_map.74 = (f32[32,64]{1,0:T(8,128)}, f32[8,64,128]{2,1,0:T(8,128)S(1)}) custom-call(s32[1]{0:T(128)} %bitcast.gx_ref, f32[128,256]{1,0:T(8,128)S(1)} %bitcast.19, f32[128,512]{1,0:T(8,128)S(1)} %get-tuple-element.17.e_ref, f32[4,16,136,128]{3,2,1,0:T(8,128)S(1)} %bitcast.17), custom_call_target="tpu_custom_call" | custom-call | tf_op jit(solution)/shard_map/pallas_call | solution.py:377
  127.9 15.1 %all_to_all.28.parts_ref = f32[128,4,128]{2,1,0:T(4,128)S(1)} all-to-all(f32[128,4,128]{2,1,0:T(4,128)S(1)} %bitcast.20), channel_id=1, replica_groups=mesh['gx'=4,'gy'=16,'gz'=2] {'gx','gy','gz'}, dimensions={0} | all-to-all | bytes 524288 | tf_op jit(solution)/shard_map/all_to_all | solution.py:415
  143.0 0.9 shard_map.75
  143.9 4.6 %all-to-all-start.4 = ((f32[128,4,128]{2,1,0:T(4,128)}), f32[128,4,128]{2,1,0:T(4,128)S(1)}, u32[]{:S(2)}, u32[]{:S(2)}) async-start(f32[128,4,128]{2,1,0:T(4,128)} %shard_map.75), calls=%async_computation.4 | async-start | bytes 524288 | tf_op jit(solution)/shard_map/all_to_all | solution.py:415
  148.5 0.1 pad_add_fusion.at_ref
  148.6 10.7 %all-to-all-done.4 = f32[128,4,128]{2,1,0:T(4,128)S(1)} async-done(((f32[128,4,128]{2,1,0:T(4,128)}), f32[128,4,128]{2,1,0:T(4,128)S(1)}, u32[]{:S(2)}, u32[]{:S(2)}) %all-to-all-start.4) | async-done | bytes 262176 | tf_op jit(solution)/shard_map/all_to_all | solution.py:415
  159.3 3.8 %shard_map.76 = f32[64,64]{1,0:T(8,128)} custom-call(s32[2]{0:T(128)S(1)} %pad_add_fusion.at_ref, f32[8,64,128]{2,1,0:T(8,128)S(1)} %bitcast.18), custom_call_target="tpu_custom_call" | custom-call | tf_op jit(solution)/shard_map/pallas_call | solution.py:405
  (1 shorter events, 0.0 us)
Async XLA Ops:
  12.8 7.1 %collective-permute-start.1 = (f32[16,4,12,8,128]{4,3,2,1,0:T(8,128)}, f32[16,4,12,8,128]{4,3,2,1,0:T(8,128)}, u32[]{:S(2)}, u32[]{:S(2)}) collective-permute-start(f32[16,4,12,8,128]{4,3,2,1,0:T(8,128)} %get-tuple-element.15), channel_id=1, source_target_pairs={{0,1},{1,0},{2,3},{3,2},{4,5},{5,4},{6,7},{7,6},{8,9},{9,8},{10,11... | collective-permute-start | bytes 9437192 | tf_op jit(solution)/shard_map/ppermute | solution.py:423
  14.3 5.6 %copy-start.1 = (f32[64,64]{1,0:T(8,128)S(1)}, f32[64,64]{1,0:T(8,128)}, u32[]{:S(2)}) copy-start(f32[64,64]{1,0:T(8,128)} %f2_ref.1) | copy-start | bytes 49156
  18.5 3.4 %collective-permute-start = (f32[16,4,4,8,128]{4,3,2,1,0:T(8,128)}, f32[16,4,4,8,128]{4,3,2,1,0:T(8,128)}, u32[]{:S(2)}, u32[]{:S(2)}) collective-permute-start(f32[16,4,4,8,128]{4,3,2,1,0:T(8,128)} %get-tuple-element.13), channel_id=1, source_target_pairs={{0,1},{1,0},{2,3},{3,2},{4,5},{5,4},{6,7},{7,6},{8,9},{9,8},{10,11... | collective-permute-start | bytes 3145736 | tf_op jit(solution)/shard_map/ppermute | solution.py:423
  19.9 2.2 %copy-start = (f32[16,4,4,8,128]{4,3,2,1,0:T(8,128)S(1)}, f32[16,4,4,8,128]{4,3,2,1,0:T(8,128)}, u32[]{:S(2)}) copy-start(f32[16,4,4,8,128]{4,3,2,1,0:T(8,128)} %get-tuple-element.12.own_ref) | copy-start | bytes 3145732
  89.0 19.4 %copy-start.2 = (f32[32,64]{1,0:T(8,128)S(1)}, f32[32,64]{1,0:T(8,128)}, u32[]{:S(2)}) copy-start(f32[32,64]{1,0:T(8,128)} %f1_ref.1) | copy-start | bytes 24580
  143.9 15.4 %all-to-all-start.4 = ((f32[128,4,128]{2,1,0:T(4,128)}), f32[128,4,128]{2,1,0:T(4,128)S(1)}, u32[]{:S(2)}, u32[]{:S(2)}) async-start(f32[128,4,128]{2,1,0:T(4,128)} %shard_map.75), calls=%async_computation.4 | async-start | bytes 524288 | tf_op jit(solution)/shard_map/all_to_all | solution.py:415

commit v5 on v4

--- a/solution.py
+++ b/solution.py
@@ -37,6 +37,10 @@
 
 def mm_f32(a, b, dims):
     return mm3(split(a), split(b), dims)
+
+
+def mm_exact(a, b, dims):
+    return lax.dot_general(a, b, dims, precision=lax.Precision.HIGHEST, preferred_element_type=F32)
 
 
 def wide(w):
@@ -248,7 +252,7 @@
         e = fp_ref[pl.ds(r, 128, stride=4), :]
         e_ref[:, r * 128 : (r + 1) * 128] = e
         eh, el = split(e)
-        gram += mm(eh, eh, NT)
+        gram += mm(eh, eh, NT) + mm(el, el, NT)
         cross += mm(eh, el, NT)
     g_ref[...] = gram + (cross + cross.T)
     group = iota((32, 128), 1) >> 5
@@ -275,7 +279,7 @@
 def rows_kernel(parts_ref, f1_ref, out_ref):
     row = jnp.sum(parts_ref[...], axis=0, keepdims=True)
     block = jnp.concatenate([row[:, i * 32 : (i + 1) * 32] for i in range(4)] * 2, 0)
-    image = mm_f32(block, f1_ref[...], NN)
+    image = mm_exact(block, f1_ref[...], NN)
     image = jnp.concatenate([image[i : i + 1] for i in range(4)], 1)
     out_ref[...] = jnp.broadcast_to(image[None], out_ref.shape)
 
@@ -291,17 +295,20 @@
 
 
 def sum_kernel(parts_ref, out_ref):
-    out_ref[...] = jnp.broadcast_to(jnp.sum(parts_ref[...], axis=0, keepdims=True), out_ref.shape)
+    total = jnp.sum(parts_ref[...], axis=0)
+    total = total + pltpu.roll(total, 4, 0)
+    out_ref[...] = jnp.broadcast_to(total[None], out_ref.shape)
 
 
 def sum_for_all(parts):
-    return pl.pallas_call(
+    total = pl.pallas_call(
         sum_kernel,
         in_specs=[VMEM],
         out_specs=VMEM,
-        out_shape=jax.ShapeDtypeStruct(parts.shape, F32),
-        compiler_params=PARAMS,
-    )(parts)
+        out_shape=jax.ShapeDtypeStruct((64, 8, 128), F32),
+        compiler_params=PARAMS,
+    )(parts.reshape(64, 8, 128))
+    return total.reshape(128, 4, 128)
 
 
 def inverse_factor(normal):
@@ -347,13 +354,13 @@
     for i in range(4):
         i_ref[pl.ds(i, 32, stride=4), :] = rows[:, i * 64 : (i + 1) * 64]
     image = i_ref[...]
-    normal = mm_f32(image, image, TN)
+    normal = mm_exact(image, image, TN)
     projected = split(mm_f32(image, e_ref[...], TN))
-    inverse = split(inverse_factor(normal))
-    basis = mm3(split(image), inverse, NT)
+    inverse = inverse_factor(normal)
+    basis = mm_exact(image, inverse, NT)
     i_ref[...] = basis * math.sqrt(128)
     new_ref[...] = i_ref[pl.ds(pl.multiple_of(32 * gx_ref[0], 32), 32), :]
-    y = mm_f32(basis, mm3(inverse, projected, NN), NN)
+    y = mm_f32(basis, mm3(split(inverse), projected, NN), NN)
     for r in range(4):
         y_ref[pl.ds(r, 128, stride=4), :] = y[:, r * 128 : (r + 1) * 128]
     yt = split(y_ref[...].T)
@@ -389,26 +396,24 @@
     )(gx, parts, e, c)
 
 
-def last_kernel(at_ref, image_ref, new_ref):
-    normal, cross = jnp.zeros((64, 64), F32), jnp.zeros((64, 64), F32)
+def last_kernel(gy_ref, image_ref, new_ref):
+    normal = jnp.zeros((64, 64), F32)
     for i in range(8):
-        h, l = split(image_ref[i])
-        normal += mm(h, h, NT)
-        cross += mm(h, l, NT)
-    inverse = inverse_factor(normal + (cross + cross.T))
-    pair = image_ref[at_ref[0]]
-    mine = jnp.where(at_ref[1] == 0, pair[:, :64], pair[:, 64:])
-    new_ref[...] = mm_f32(mine, inverse, (((0,), (1,)), ((), ()))) * math.sqrt(1024)
-
-
-def last_factor(at, image):
+        normal += mm_exact(image_ref[i], image_ref[i], NT)
+    inverse = inverse_factor(normal)
+    pair = image_ref[gy_ref[0] >> 1]
+    mine = jnp.where(gy_ref[0] & 1 == 0, pair[:, :64], pair[:, 64:])
+    new_ref[...] = mm_exact(mine.T, inverse, NT) * math.sqrt(1024)
+
+
+def last_factor(gy, image):
     return pl.pallas_call(
         last_kernel,
         in_specs=[SMEM, VMEM],
         out_specs=VMEM,
         out_shape=jax.ShapeDtypeStruct((64, 64), F32),
         compiler_params=PARAMS,
-    )(at, image)
+    )(gy, image)
 
 
 def to_all(x, names=ALL):
@@ -438,7 +443,7 @@
     rows = image_rows(to_all(gram.reshape(128, 1, 128)).reshape(128, 128), factor_one)
     new_one, second_part = second_image(gx[None], to_all(rows).reshape(128, 256), e, c)
     second = to_all(sum_for_all(to_all(second_part.reshape(128, 4, 128)))).reshape(8, 64, 128)
-    new_two = last_factor(jnp.stack([gy // 2, gy % 2]), second)
+    new_two = last_factor(gy[None], second)
     return new_one, new_two
 
 

time: 163 us -> 163 us (level)
  no operation moved by 1% of the time
where the time goes in v5:
time: 163 us
  blocking collectives  112 us (69%)
  Pallas kernels  30.6 us (19%)
  waiting for transfers between devices  12.1 us (7%)
  starting transfers between devices  6.25 us (4%)
    all_to_all x4, blocking collectives, to_all(): return lax.all_to_all(x, names, 0, 0, tiled=True)  112 us
    pallas_call x2, Pallas kernels, core_cut(): pl.pallas_call(functools.partial(core_kernel, chunk), in_specs=[SMEM, HBM...  15.5 us
    all_to_all x1, waiting for transfers between devices, to_all(): return lax.all_to_all(x, names, 0, 0, tiled=True)  10.8 us
    pallas_call x1, Pallas kernels, second_image(): pl.pallas_call(second_kernel, in_specs=[SMEM, VMEM, VMEM, HBM], out_specs...  4.78 us
    all_to_all x1, starting transfers between devices, to_all(): return lax.all_to_all(x, names, 0, 0, tiled=True)  4.65 us
    pallas_call x1, Pallas kernels, last_factor(): pl.pallas_call(last_kernel, in_specs=[SMEM, VMEM], out_specs=VMEM, out_sh...  3.51 us
  transfers between devices with their start and end apart: 3, of which 2 were waited for; matrix products, arithmetic and copies ran while one was open for 0% of the time, Pallas kernels for 4%

profile of v5, /device:TPU:1, one launch (start us, length us, event | category | flops | bytes accessed | tf_op | source)
XLA Modules:
  0.0 163.0 jit_solution(10670996830620970371)
XLA Ops:
  0.6 0.9 select_maximum_fusion.factors_ref
  1.5 11.3 %shard_map.68 = (f32[16,4,12,8,128]{4,3,2,1,0:T(8,128)S(1)}, f32[16,4,12,8,128]{4,3,2,1,0:T(8,128)}, f32[4,64,32,64]{3,2,1,0:T(8,128)S(1)}) custom-call(s32[1]{0:T(128)} %bitcast.1.gz_ref, f32[32,64,32,64]{3,2,1,0:T(8,128)} %bitcast.25, f32[64,128]{1,0:T(8,128)S(1)} %select_maximum_fusion.factors_ref), custom_call_target="tpu_custom_call" | custom-call | tf_op jit(solution)/shard_map/pallas_call | solution.py:173
  12.8 1.5 collective-permute-start.1
  14.3 0.0 copy-start.1
  14.3 4.2 %shard_map.69 = (f32[16,4,4,8,128]{4,3,2,1,0:T(8,128)}, f32[16,4,4,8,128]{4,3,2,1,0:T(8,128)}) custom-call(s32[1]{0:T(128)} %bitcast.1.gz_ref, f32[32,64,32,64]{3,2,1,0:T(8,128)} %bitcast.26, f32[64,128]{1,0:T(8,128)S(1)} %select_maximum_fusion.factors_ref, f32[4,64,32,64]{3,2,1,0:T(8,128)S(1)} %get-tuple-element.11.rest_0_), custom_call_target="tpu_custom_call" | custom-call | tf_op jit(solution)/shard_map/pallas_call | solution.py:173
  18.5 0.1 collective-permute-start
  18.6 1.3 collective-permute-done.1.other_hbm
  19.9 0.0 copy-done.1
  19.9 0.0 copy-start
  19.9 2.0 %shard_map.70.sent_ref = f32[64,136,128]{2,1,0:T(8,128)S(1)} custom-call(s32[1]{0:T(128)} %bitcast.gx_ref, f32[16,4,12,8,128]{4,3,2,1,0:T(8,128)S(1)} %get-tuple-element.14.own_ref, f32[16,4,12,8,128]{4,3,2,1,0:T(8,128)} %collective-permute-done.1.other_hbm, f32[64,64]{1,0:T(8,128)S(1)} %copy-done.1), custom_call_target="tpu_custom_call" | custom-call | tf_op jit(solution)/shard_map/pallas_call | solution.py:216
  22.0 0.0 collective-permute-done.other_ref
  22.0 0.1 copy-done
  22.1 1.3 shard_map.71
  23.4 65.5 %all_to_all.25 = f32[64,136,128]{2,1,0:T(8,128)S(1)} all-to-all(f32[64,136,128]{2,1,0:T(8,128)S(1)} %shard_map.71), channel_id=1, replica_groups=mesh['gx'=4,'gy'=16,'gz'=2] {'gx','gy'}, dimensions={0} | all-to-all | bytes 8912896 | tf_op jit(solution)/shard_map/all_to_all | solution.py:420
  89.0 0.0 copy-start.2
  89.0 2.3 %shard_map.72 = (f32[128,512]{1,0:T(8,128)S(1)}, f32[4,32,128]{2,1,0:T(8,128)S(1)}) custom-call(f32[4,16,136,128]{3,2,1,0:T(8,128)S(1)} %bitcast.17), custom_call_target="tpu_custom_call" | custom-call | tf_op jit(solution)/shard_map/pallas_call | solution.py:269
  91.2 17.3 %all_to_all.26 = f32[128,1,128]{2,1,0:T(1,128)S(1)} all-to-all(f32[128,1,128]{2,1,0:T(1,128)S(1)} %bitcast.24), channel_id=1, replica_groups=mesh['gx'=4,'gy'=16,'gz'=2] {'gx','gy','gz'}, dimensions={0} | all-to-all | bytes 131072 | tf_op jit(solution)/shard_map/all_to_all | solution.py:420
  108.5 0.0 copy-done.2
  108.5 0.3 shard_map.73
  108.8 14.5 %all_to_all.27 = f32[128,1,256]{2,1,0:T(1,128)S(1)} all-to-all(f32[128,1,256]{2,1,0:T(1,128)S(1)} %shard_map.73), channel_id=1, replica_groups=mesh['gx'=4,'gy'=16,'gz'=2] {'gx','gy','gz'}, dimensions={0} | all-to-all | bytes 262144 | tf_op jit(solution)/shard_map/all_to_all | solution.py:420
  123.3 4.8 %shard_map.74 = (f32[32,64]{1,0:T(8,128)}, f32[8,64,128]{2,1,0:T(8,128)S(1)}) custom-call(s32[1]{0:T(128)} %bitcast.gx_ref, f32[128,256]{1,0:T(8,128)S(1)} %bitcast.21, f32[128,512]{1,0:T(8,128)S(1)} %get-tuple-element.17.e_ref, f32[4,16,136,128]{3,2,1,0:T(8,128)S(1)} %bitcast.18), custom_call_target="tpu_custom_call" | custom-call | tf_op jit(solution)/shard_map/pallas_call | solution.py:384
  128.1 15.1 %all_to_all.28 = f32[128,4,128]{2,1,0:T(4,128)S(1)} all-to-all(f32[128,4,128]{2,1,0:T(4,128)S(1)} %bitcast.22), channel_id=1, replica_groups=mesh['gx'=4,'gy'=16,'gz'=2] {'gx','gy','gz'}, dimensions={0} | all-to-all | bytes 524288 | tf_op jit(solution)/shard_map/all_to_all | solution.py:420
  143.2 0.8 shard_map.75
  144.0 4.6 %all-to-all-start.4 = ((f32[128,4,128]{2,1,0:T(4,128)}), f32[128,4,128]{2,1,0:T(4,128)S(1)}, u32[]{:S(2)}, u32[]{:S(2)}) async-start(f32[128,4,128]{2,1,0:T(4,128)} %bitcast.11), calls=%async_computation.4 | async-start | bytes 524288 | tf_op jit(solution)/shard_map/all_to_all | solution.py:420
  148.7 10.8 %all-to-all-done.4 = f32[128,4,128]{2,1,0:T(4,128)S(1)} async-done(((f32[128,4,128]{2,1,0:T(4,128)}), f32[128,4,128]{2,1,0:T(4,128)S(1)}, u32[]{:S(2)}, u32[]{:S(2)}) %all-to-all-start.4) | async-done | bytes 262176 | tf_op jit(solution)/shard_map/all_to_all | solution.py:420
  159.5 3.5 %shard_map.76 = f32[64,64]{1,0:T(8,128)} custom-call(s32[1]{0:T(128)} %bitcast.8.gy_ref, f32[8,64,128]{2,1,0:T(8,128)S(1)} %bitcast.19), custom_call_target="tpu_custom_call" | custom-call | tf_op jit(solution)/shard_map/pallas_call | solution.py:410
  (1 shorter events, 0.0 us)
Async XLA Ops:
  12.8 7.1 %collective-permute-start.1 = (f32[16,4,12,8,128]{4,3,2,1,0:T(8,128)}, f32[16,4,12,8,128]{4,3,2,1,0:T(8,128)}, u32[]{:S(2)}, u32[]{:S(2)}) collective-permute-start(f32[16,4,12,8,128]{4,3,2,1,0:T(8,128)} %get-tuple-element.15), channel_id=1, source_target_pairs={{0,1},{1,0},{2,3},{3,2},{4,5},{5,4},{6,7},{7,6},{8,9},{9,8},{10,11... | collective-permute-start | bytes 9437192 | tf_op jit(solution)/shard_map/ppermute | solution.py:428
  14.3 5.6 %copy-start.1 = (f32[64,64]{1,0:T(8,128)S(1)}, f32[64,64]{1,0:T(8,128)}, u32[]{:S(2)}) copy-start(f32[64,64]{1,0:T(8,128)} %f2_ref.1) | copy-start | bytes 49156
  18.5 3.4 %collective-permute-start = (f32[16,4,4,8,128]{4,3,2,1,0:T(8,128)}, f32[16,4,4,8,128]{4,3,2,1,0:T(8,128)}, u32[]{:S(2)}, u32[]{:S(2)}) collective-permute-start(f32[16,4,4,8,128]{4,3,2,1,0:T(8,128)} %get-tuple-element.13), channel_id=1, source_target_pairs={{0,1},{1,0},{2,3},{3,2},{4,5},{5,4},{6,7},{7,6},{8,9},{9,8},{10,11... | collective-permute-start | bytes 3145736 | tf_op jit(solution)/shard_map/ppermute | solution.py:428
  19.9 2.2 %copy-start = (f32[16,4,4,8,128]{4,3,2,1,0:T(8,128)S(1)}, f32[16,4,4,8,128]{4,3,2,1,0:T(8,128)}, u32[]{:S(2)}) copy-start(f32[16,4,4,8,128]{4,3,2,1,0:T(8,128)} %get-tuple-element.12.own_ref) | copy-start | bytes 3145732
  89.0 19.6 %copy-start.2 = (f32[32,64]{1,0:T(8,128)S(1)}, f32[32,64]{1,0:T(8,128)}, u32[]{:S(2)}) copy-start(f32[32,64]{1,0:T(8,128)} %f1_ref.1) | copy-start | bytes 24580
  144.0 15.4 %all-to-all-start.4 = ((f32[128,4,128]{2,1,0:T(4,128)}), f32[128,4,128]{2,1,0:T(4,128)S(1)}, u32[]{:S(2)}, u32[]{:S(2)}) async-start(f32[128,4,128]{2,1,0:T(4,128)} %bitcast.11), calls=%async_computation.4 | async-start | bytes 524288 | tf_op jit(solution)/shard_map/all_to_all | solution.py:420

commit v6 on v5

--- a/solution.py
+++ b/solution.py
@@ -205,9 +205,17 @@
         out_ref[4 * g : 4 * g + 4, :rows] = (own_ref[g] + other_ref[g]).reshape(4, rows, 128)
 
 
-def merge_second_kernel(own_ref, other_ref, sent_ref, out_ref):
+def merge_second_kernel(own_ref, other_hbm, sent_ref, out_ref, other_ref, sems):
     rows = 8 * PAIRS[1]
+    copies = [
+        pltpu.make_async_copy(other_hbm.at[pl.ds(4 * g, 4)], other_ref.at[pl.ds(4 * g, 4)], sems.at[g])
+        for g in range(4)
+    ]
+    for copy in copies:
+        copy.start()
     for g in range(16):
+        if g % 4 == 0:
+            copies[g // 4].wait()
         total = (own_ref[g] + other_ref[g]).reshape(4, rows, 128)
         out_ref[4 * g : 4 * g + 4, 8 * PAIRS[0] : 128] = total
 
@@ -226,12 +234,13 @@
 def merge_second(own, other, sent):
     return pl.pallas_call(
         merge_second_kernel,
-        in_specs=[VMEM, VMEM, VMEM],
+        in_specs=[VMEM, HBM, VMEM],
         out_specs=VMEM,
         out_shape=pltpu.VMEM((64, 136, 128), F32),
+        scratch_shapes=[pltpu.VMEM(other.shape, F32), pltpu.SemaphoreType.DMA((4,))],
         input_output_aliases={2: 0},
         compiler_params=PARAMS,
-    )(own, other, sent)
+    )(own, in_hbm(other), sent)
 
 
 def first_kernel(c_ref, e_ref, gram_ref, fp_ref, g_ref):

time: 163 us -> 163 us (level)
  no operation moved by 1% of the time
where the time goes in v6:
time: 163 us
  blocking collectives  112 us (69%)
  Pallas kernels  30.5 us (19%)
  waiting for transfers between devices  12.1 us (7%)
  starting transfers between devices  6.25 us (4%)
    all_to_all x4, blocking collectives, to_all(): return lax.all_to_all(x, names, 0, 0, tiled=True)  112 us
    pallas_call x2, Pallas kernels, core_cut(): pl.pallas_call(functools.partial(core_kernel, chunk), in_specs=[SMEM, HBM...  15.5 us
    all_to_all x1, waiting for transfers between devices, to_all(): return lax.all_to_all(x, names, 0, 0, tiled=True)  10.8 us
    pallas_call x1, Pallas kernels, second_image(): pl.pallas_call(second_kernel, in_specs=[SMEM, VMEM, VMEM, HBM], out_specs...  4.78 us
    all_to_all x1, starting transfers between devices, to_all(): return lax.all_to_all(x, names, 0, 0, tiled=True)  4.65 us
    pallas_call x1, Pallas kernels, last_factor(): pl.pallas_call(last_kernel, in_specs=[SMEM, VMEM], out_specs=VMEM, out_sh...  3.51 us
  transfers between devices with their start and end apart: 3, of which 2 were waited for; matrix products, arithmetic and copies ran while one was open for 0% of the time, Pallas kernels for 4%

profile of v6, /device:TPU:1, one launch (start us, length us, event | category | flops | bytes accessed | tf_op | source)
XLA Modules:
  0.0 162.9 jit_solution(6099342696586189028)
XLA Ops:
  0.6 0.9 select_maximum_fusion.factors_ref
  1.5 11.3 %shard_map.68 = (f32[16,4,12,8,128]{4,3,2,1,0:T(8,128)S(1)}, f32[16,4,12,8,128]{4,3,2,1,0:T(8,128)}, f32[4,64,32,64]{3,2,1,0:T(8,128)S(1)}) custom-call(s32[1]{0:T(128)} %bitcast.1.gz_ref, f32[32,64,32,64]{3,2,1,0:T(8,128)} %bitcast.25, f32[64,128]{1,0:T(8,128)S(1)} %select_maximum_fusion.factors_ref), custom_call_target="tpu_custom_call" | custom-call | tf_op jit(solution)/shard_map/pallas_call | solution.py:173
  12.8 1.5 collective-permute-start.1
  14.3 0.0 copy-start.1
  14.3 4.2 %shard_map.69 = (f32[16,4,4,8,128]{4,3,2,1,0:T(8,128)}, f32[16,4,4,8,128]{4,3,2,1,0:T(8,128)}) custom-call(s32[1]{0:T(128)} %bitcast.1.gz_ref, f32[32,64,32,64]{3,2,1,0:T(8,128)} %bitcast.26, f32[64,128]{1,0:T(8,128)S(1)} %select_maximum_fusion.factors_ref, f32[4,64,32,64]{3,2,1,0:T(8,128)S(1)} %get-tuple-element.11.rest_0_), custom_call_target="tpu_custom_call" | custom-call | tf_op jit(solution)/shard_map/pallas_call | solution.py:173
  18.5 0.1 collective-permute-start
  18.6 1.3 collective-permute-done.1.other_hbm
  19.9 0.0 copy-done.1
  19.9 0.0 copy-start
  19.9 2.0 %shard_map.70.sent_ref = f32[64,136,128]{2,1,0:T(8,128)S(1)} custom-call(s32[1]{0:T(128)} %bitcast.gx_ref, f32[16,4,12,8,128]{4,3,2,1,0:T(8,128)S(1)} %get-tuple-element.14.own_ref, f32[16,4,12,8,128]{4,3,2,1,0:T(8,128)} %collective-permute-done.1.other_hbm, f32[64,64]{1,0:T(8,128)S(1)} %copy-done.1), custom_call_target="tpu_custom_call" | custom-call | tf_op jit(solution)/shard_map/pallas_call | solution.py:224
  22.0 0.0 collective-permute-done.other_hbm
  22.0 0.1 copy-done
  22.1 1.2 shard_map.71
  23.4 65.5 %all_to_all.25 = f32[64,136,128]{2,1,0:T(8,128)S(1)} all-to-all(f32[64,136,128]{2,1,0:T(8,128)S(1)} %shard_map.71), channel_id=1, replica_groups=mesh['gx'=4,'gy'=16,'gz'=2] {'gx','gy'}, dimensions={0} | all-to-all | bytes 8912896 | tf_op jit(solution)/shard_map/all_to_all | solution.py:429
  88.9 0.0 copy-start.2
  88.9 2.3 %shard_map.72 = (f32[128,512]{1,0:T(8,128)S(1)}, f32[4,32,128]{2,1,0:T(8,128)S(1)}) custom-call(f32[4,16,136,128]{3,2,1,0:T(8,128)S(1)} %bitcast.17), custom_call_target="tpu_custom_call" | custom-call | tf_op jit(solution)/shard_map/pallas_call | solution.py:278
  91.2 17.2 %all_to_all.26 = f32[128,1,128]{2,1,0:T(1,128)S(1)} all-to-all(f32[128,1,128]{2,1,0:T(1,128)S(1)} %bitcast.24), channel_id=1, replica_groups=mesh['gx'=4,'gy'=16,'gz'=2] {'gx','gy','gz'}, dimensions={0} | all-to-all | bytes 131072 | tf_op jit(solution)/shard_map/all_to_all | solution.py:429
  108.4 0.0 copy-done.2
  108.4 0.3 shard_map.73
  108.8 14.5 %all_to_all.27 = f32[128,1,256]{2,1,0:T(1,128)S(1)} all-to-all(f32[128,1,256]{2,1,0:T(1,128)S(1)} %shard_map.73), channel_id=1, replica_groups=mesh['gx'=4,'gy'=16,'gz'=2] {'gx','gy','gz'}, dimensions={0} | all-to-all | bytes 262144 | tf_op jit(solution)/shard_map/all_to_all | solution.py:429
  123.2 4.8 %shard_map.74 = (f32[32,64]{1,0:T(8,128)}, f32[8,64,128]{2,1,0:T(8,128)S(1)}) custom-call(s32[1]{0:T(128)} %bitcast.gx_ref, f32[128,256]{1,0:T(8,128)S(1)} %bitcast.21, f32[128,512]{1,0:T(8,128)S(1)} %get-tuple-element.17.e_ref, f32[4,16,136,128]{3,2,1,0:T(8,128)S(1)} %bitcast.18), custom_call_target="tpu_custom_call" | custom-call | tf_op jit(solution)/shard_map/pallas_call | solution.py:393
  128.0 15.1 %all_to_all.28 = f32[128,4,128]{2,1,0:T(4,128)S(1)} all-to-all(f32[128,4,128]{2,1,0:T(4,128)S(1)} %bitcast.22), channel_id=1, replica_groups=mesh['gx'=4,'gy'=16,'gz'=2] {'gx','gy','gz'}, dimensions={0} | all-to-all | bytes 524288 | tf_op jit(solution)/shard_map/all_to_all | solution.py:429
  143.2 0.8 shard_map.75
  144.0 4.6 %all-to-all-start.4 = ((f32[128,4,128]{2,1,0:T(4,128)}), f32[128,4,128]{2,1,0:T(4,128)S(1)}, u32[]{:S(2)}, u32[]{:S(2)}) async-start(f32[128,4,128]{2,1,0:T(4,128)} %bitcast.11), calls=%async_computation.4 | async-start | bytes 524288 | tf_op jit(solution)/shard_map/all_to_all | solution.py:429
  148.6 10.8 %all-to-all-done.4 = f32[128,4,128]{2,1,0:T(4,128)S(1)} async-done(((f32[128,4,128]{2,1,0:T(4,128)}), f32[128,4,128]{2,1,0:T(4,128)S(1)}, u32[]{:S(2)}, u32[]{:S(2)}) %all-to-all-start.4) | async-done | bytes 262176 | tf_op jit(solution)/shard_map/all_to_all | solution.py:429
  159.4 3.5 %shard_map.76 = f32[64,64]{1,0:T(8,128)} custom-call(s32[1]{0:T(128)} %bitcast.8.gy_ref, f32[8,64,128]{2,1,0:T(8,128)S(1)} %bitcast.19), custom_call_target="tpu_custom_call" | custom-call | tf_op jit(solution)/shard_map/pallas_call | solution.py:419
  (1 shorter events, 0.0 us)
Async XLA Ops:
  12.8 7.1 %collective-permute-start.1 = (f32[16,4,12,8,128]{4,3,2,1,0:T(8,128)}, f32[16,4,12,8,128]{4,3,2,1,0:T(8,128)}, u32[]{:S(2)}, u32[]{:S(2)}) collective-permute-start(f32[16,4,12,8,128]{4,3,2,1,0:T(8,128)} %get-tuple-element.15), channel_id=1, source_target_pairs={{0,1},{1,0},{2,3},{3,2},{4,5},{5,4},{6,7},{7,6},{8,9},{9,8},{10,11... | collective-permute-start | bytes 9437192 | tf_op jit(solution)/shard_map/ppermute | solution.py:437
  14.3 5.6 %copy-start.1 = (f32[64,64]{1,0:T(8,128)S(1)}, f32[64,64]{1,0:T(8,128)}, u32[]{:S(2)}) copy-start(f32[64,64]{1,0:T(8,128)} %f2_ref.1) | copy-start | bytes 49156
  18.5 3.4 %collective-permute-start = (f32[16,4,4,8,128]{4,3,2,1,0:T(8,128)}, f32[16,4,4,8,128]{4,3,2,1,0:T(8,128)}, u32[]{:S(2)}, u32[]{:S(2)}) collective-permute-start(f32[16,4,4,8,128]{4,3,2,1,0:T(8,128)} %get-tuple-element.13), channel_id=1, source_target_pairs={{0,1},{1,0},{2,3},{3,2},{4,5},{5,4},{6,7},{7,6},{8,9},{9,8},{10,11... | collective-permute-start | bytes 3145736 | tf_op jit(solution)/shard_map/ppermute | solution.py:437
  19.9 2.2 %copy-start = (f32[16,4,4,8,128]{4,3,2,1,0:T(8,128)S(1)}, f32[16,4,4,8,128]{4,3,2,1,0:T(8,128)}, u32[]{:S(2)}) copy-start(f32[16,4,4,8,128]{4,3,2,1,0:T(8,128)} %get-tuple-element.12.own_ref) | copy-start | bytes 3145732
  88.9 19.5 %copy-start.2 = (f32[32,64]{1,0:T(8,128)S(1)}, f32[32,64]{1,0:T(8,128)}, u32[]{:S(2)}) copy-start(f32[32,64]{1,0:T(8,128)} %f1_ref.1) | copy-start | bytes 24580
  144.0 15.4 %all-to-all-start.4 = ((f32[128,4,128]{2,1,0:T(4,128)}), f32[128,4,128]{2,1,0:T(4,128)S(1)}, u32[]{:S(2)}, u32[]{:S(2)}) async-start(f32[128,4,128]{2,1,0:T(4,128)} %bitcast.11), calls=%async_computation.4 | async-start | bytes 524288 | tf_op jit(solution)/shard_map/all_to_all | solution.py:429
